TPU v7x, 512 devices: a whole 4x8x8 slice. The times are simulated.
512 devices in a mesh: filt: 4 (over z_hi, core), il: 32 (over z_lo, y), xl: 4 (over x).
Axes of the slice: x: 4, y: 8, z: 8 (z_hi: 2, z_lo: 4; z = z_hi * 4 + z_lo), core: 2. Of those that a mesh axis runs over, the one named last changes fastest.
Arguments:
- baseline: float32 [4, 32, 64, 512], P(None, 'il', 'xl', 'filt'), may hold values from -6 to 6
- monitor: float32 [4, 32, 64, 512], P(None, 'il', 'xl', 'filt'), may hold values from -6 to 6
- band_ids: int32 [4, 32, 8, 2], P(None, 'il', 'xl'), may hold values from 0 to 15, all different within a row
- quality: float32 [4, 32, 64, 512], P('filt', 'il', 'xl'), may hold values from 0.25 to 2
Outputs:
- shift: float32 [4, 32, 64, 512], P('filt', 'il', 'xl')
- residual: float32 [4, 32, 64, 512], P('filt', 'il', 'xl')
Inputs may be any that keep to these rules, and one draw needn't show every extreme that they name: `band_ids`: the 2 bands of each trace block of 8 crossline traces are distinct; band b covers lags b * 8 - 64 to b * 8 - 57.
All inputs are finite; a program needn't handle non-finite values.
Results may differ from a plain program's by a relative error of at most 0.00056.
Values may be sent and summed in bfloat16 or wider, within the bound.
No kernel may reach another device: no remote copies, remote signals or barrier semaphores. Data moves between devices by JAX's collectives and lax.ppermute only.
A program may use at most 64 MiB of HBM per device.

v0:
```python
import jax
import jax.numpy as jnp
from jax import lax
from jax.sharding import PartitionSpec as P

BAND = 8
KB = 2
BXL = 8
ITERS = 8
LAGS = 128
HALF = 64


smooth_space = 4.0
smooth_time = 1.0


def padded_2(value, sides, width):
    for axis, dim in sides:
        size, length = (lax.axis_size(axis), value.shape[dim])
        up = [(i, (i + 1) % size) for i in range(size - 1)]
        down = [(j, i) for i, j in up]
        last = lax.slice_in_dim(value, length - width, length, axis=dim)
        first = lax.slice_in_dim(value, 0, width, axis=dim)
        before = lax.ppermute(last, axis, up)
        after = lax.ppermute(first, axis, down)
        value = jnp.concatenate([before, value, after], axis=dim)
    return value


def slot_window(block, band):
    start = band * BAND
    return lax.dynamic_slice(
        block, (jnp.int32(0), start), (block.shape[0], block.shape[1] - LAGS + BAND)
    )


def lag_table(band_list):
    steps = jnp.arange(BAND, dtype=jnp.float32)
    return (band_list.astype(jnp.float32)[..., None] * BAND + steps - HALF) / HALF


def moments(errors, lags):
    likeness = 1.0 / (1.0 + errors.astype(jnp.float32))
    weight_sum = jnp.sum(likeness, axis=(3, 4)) / (KB * BAND)
    moment_sum = jnp.sum(lags[..., None, None] * likeness, axis=(3, 4)) / (KB * BAND)
    return (weight_sum, moment_sum)


def operate(field, weight):
    padded = padded_2(field, ((("filt", "il"), 0), ("xl", 1)), 1)
    centre = padded[1:-1, 1:-1, :]
    across = (
        4.0 * centre
        - padded[2:, 1:-1, :]
        - padded[:-2, 1:-1, :]
        - padded[1:-1, 2:, :]
        - padded[1:-1, :-2, :]
    )
    timed = jnp.pad(field, ((0, 0), (0, 0), (1, 1)))
    along = 2.0 * field - timed[:, :, 2:] - timed[:, :, :-2]
    return weight * field + smooth_space * across + smooth_time * along


def squares(residual):
    return lax.psum(jnp.sum(residual * residual), ("filt", "il", "xl"))


def per_device(baseline, monitor, band_ids, quality):
    quarters, inline_rows, cross_rows, samples = baseline.shape
    cross_blocks = cross_rows // BXL
    extended = padded_2(monitor, (("filt", 3),), HALF)
    ext_blocks = extended.reshape(quarters, inline_rows, cross_blocks, BXL, samples + LAGS)
    base_blocks = baseline.reshape(quarters, inline_rows, cross_blocks, BXL, samples)
    per_slot = jax.vmap(slot_window, in_axes=(None, 0))
    windows = jax.vmap(jax.vmap(jax.vmap(per_slot)))(ext_blocks, band_ids)
    errors = jnp.stack(
        [
            jnp.square(
                base_blocks[:, :, :, None] - windows[..., lag_step : lag_step + samples]
            ).astype(jnp.bfloat16)
            for lag_step in range(BAND)
        ],
        axis=4,
    )
    local_weight, local_moment = moments(errors, lag_table(band_ids))
    weight_raw, moment_raw = (
        lax.all_to_all(local_weight, "filt", split_axis=0, concat_axis=4, tiled=True),
        lax.all_to_all(local_moment, "filt", split_axis=0, concat_axis=4, tiled=True),
    )
    total_time = weight_raw.shape[-1]
    quality_grid = quality.reshape(inline_rows, cross_rows, total_time)
    weight = quality_grid * weight_raw.reshape(inline_rows, cross_rows, total_time)
    target = quality_grid * moment_raw.reshape(inline_rows, cross_rows, total_time)
    shift = jnp.zeros_like(target)
    residual = target
    direction = target
    norm_now = squares(residual)
    for iteration in range(ITERS):
        image = operate(direction, weight)
        alpha = norm_now / lax.psum(jnp.sum(direction * image), ("filt", "il", "xl"))
        shift = shift + alpha * direction
        residual = residual - alpha * image
        norm_next = squares(residual)
        direction = residual + norm_next / norm_now * direction
        norm_now = norm_next
    out_shape = (1, inline_rows, cross_rows, total_time)
    return (shift.reshape(out_shape), residual.reshape(out_shape))


def solution(mesh):
    in_specs = (
        P(None, "il", "xl", "filt"),
        P(None, "il", "xl", "filt"),
        P(None, "il", "xl", None),
        P("filt", "il", "xl", None),
    )
    out_specs = (P("filt", "il", "xl", None), P("filt", "il", "xl", None))
    return jax.shard_map(
        per_device, mesh=mesh, in_specs=in_specs, out_specs=out_specs, check_vma=False
    )
```

profile of v0, /device:TPU:1, one launch (start us, length us, event | category | flops | bytes accessed | tf_op | source)
XLA Modules:
  0.0 1662.0 jit_solution(16006573584481964588)
XLA Ops:
  1.5 12.0 collective-permute-start
  13.6 1.9 collective-permute-start.1
  17.4 5.3 collective-permute-done.1
  24.3 2.2 gather_fusion
  26.6 5.1 fusion.92
  31.6 1.5 copy.105
  33.1 1.4 copy.106
  34.9 1.5 copy.108
  36.4 1.4 copy.109
  40.2 8.9 all_to_all.30
  49.1 8.5 collective-permute-start.2
  57.6 1.9 collective-permute-start.3
  60.8 3.7 all-to-all-start.1
  64.4 2.2 collective-permute-done.3
  66.7 1.3 collective-permute-start.4
  68.0 4.0 collective-permute-start.5
  73.5 99.8 %all-reduce.9 = (f32[]{:T(128)}, f32[]{:T(128)}) all-reduce(f32[]{:T(128)} %get-tuple-element.5, f32[]{:T(128)} %get-tuple-element.4), channel_id=1, replica_groups=mesh['filt'=4,'il'=32,'xl'=4] {'filt','il','xl'}, use_global_device_ids=true, to_apply=%region_2.0 | all-reduce | flops 2 | bytes 16 | tf_op jit(solution)/shard_map/psum | solution.py:66
  175.2 93.5 %psum.114 = f32[]{:T(128)} all-reduce(f32[]{:T(128)} %multiply_reduce_fusion.14), channel_id=1, replica_groups=mesh['filt'=4,'il'=32,'xl'=4] {'filt','il','xl'}, use_global_device_ids=true, to_apply=%region_7.8 | all-reduce | flops 1 | bytes 8 | tf_op jit(solution)/shard_map/psum | solution.py:66
  270.1 3.3 collective-permute-start.6
  273.4 2.0 collective-permute-start.7
  275.4 7.2 collective-permute-done.7
  282.6 1.3 collective-permute-start.8
  283.9 4.3 collective-permute-start.9
  289.7 95.9 %psum.115 = f32[]{:T(128)} all-reduce(f32[]{:T(128)} %get-tuple-element.32), channel_id=1, replica_groups=mesh['filt'=4,'il'=32,'xl'=4] {'filt','il','xl'}, use_global_device_ids=true, to_apply=%region_9.10 | all-reduce | flops 1 | bytes 8 | tf_op jit(solution)/shard_map/psum | solution.py:101
  387.5 94.4 %psum.116 = f32[]{:T(128)} all-reduce(f32[]{:T(128)} %get-tuple-element.30), channel_id=1, replica_groups=mesh['filt'=4,'il'=32,'xl'=4] {'filt','il','xl'}, use_global_device_ids=true, to_apply=%region_11.12 | all-reduce | flops 1 | bytes 8 | tf_op jit(solution)/shard_map/psum | solution.py:66
  483.2 3.3 collective-permute-start.10
  486.6 2.0 collective-permute-start.11
  488.5 7.2 collective-permute-done.11
  495.7 1.3 collective-permute-start.12
  497.0 4.0 collective-permute-start.13
  502.5 94.5 %psum.117 = f32[]{:T(128)} all-reduce(f32[]{:T(128)} %get-tuple-element.28), channel_id=1, replica_groups=mesh['filt'=4,'il'=32,'xl'=4] {'filt','il','xl'}, use_global_device_ids=true, to_apply=%region_13.14 | all-reduce | flops 1 | bytes 8 | tf_op jit(solution)/shard_map/psum | solution.py:101
  598.9 94.8 %psum.118 = f32[]{:T(128)} all-reduce(f32[]{:T(128)} %get-tuple-element.26), channel_id=1, replica_groups=mesh['filt'=4,'il'=32,'xl'=4] {'filt','il','xl'}, use_global_device_ids=true, to_apply=%region_15.16 | all-reduce | flops 1 | bytes 8 | tf_op jit(solution)/shard_map/psum | solution.py:66
  695.1 4.3 collective-permute-start.14
  699.4 1.9 collective-permute-start.15
  701.4 7.2 collective-permute-done.15
  708.6 1.3 collective-permute-start.16
  709.9 4.0 collective-permute-start.17
  715.3 94.2 %psum.119 = f32[]{:T(128)} all-reduce(f32[]{:T(128)} %get-tuple-element.24), channel_id=1, replica_groups=mesh['filt'=4,'il'=32,'xl'=4] {'filt','il','xl'}, use_global_device_ids=true, to_apply=%region_17.18 | all-reduce | flops 1 | bytes 8 | tf_op jit(solution)/shard_map/psum | solution.py:101
  811.4 94.1 %psum.120 = f32[]{:T(128)} all-reduce(f32[]{:T(128)} %get-tuple-element.22), channel_id=1, replica_groups=mesh['filt'=4,'il'=32,'xl'=4] {'filt','il','xl'}, use_global_device_ids=true, to_apply=%region_19.20 | all-reduce | flops 1 | bytes 8 | tf_op jit(solution)/shard_map/psum | solution.py:66
  906.9 4.5 collective-permute-start.18
  911.4 1.9 collective-permute-start.19
  913.4 7.2 collective-permute-done.19
  920.6 1.3 collective-permute-start.20
  921.9 4.0 collective-permute-start.21
  927.3 94.3 %psum.121 = f32[]{:T(128)} all-reduce(f32[]{:T(128)} %get-tuple-element.20), channel_id=1, replica_groups=mesh['filt'=4,'il'=32,'xl'=4] {'filt','il','xl'}, use_global_device_ids=true, to_apply=%region_21.22 | all-reduce | flops 1 | bytes 8 | tf_op jit(solution)/shard_map/psum | solution.py:101
  1023.5 94.3 %psum.122 = f32[]{:T(128)} all-reduce(f32[]{:T(128)} %get-tuple-element.18), channel_id=1, replica_groups=mesh['filt'=4,'il'=32,'xl'=4] {'filt','il','xl'}, use_global_device_ids=true, to_apply=%region_23.24 | all-reduce | flops 1 | bytes 8 | tf_op jit(solution)/shard_map/psum | solution.py:66
  1119.2 4.6 collective-permute-start.22
  1123.8 1.9 collective-permute-start.23
  1125.7 7.2 collective-permute-done.23
  1132.9 1.3 collective-permute-start.24
  1134.2 4.0 collective-permute-start.25
  1139.7 94.2 %psum.123 = f32[]{:T(128)} all-reduce(f32[]{:T(128)} %get-tuple-element.16), channel_id=1, replica_groups=mesh['filt'=4,'il'=32,'xl'=4] {'filt','il','xl'}, use_global_device_ids=true, to_apply=%region_25.26 | all-reduce | flops 1 | bytes 8 | tf_op jit(solution)/shard_map/psum | solution.py:101
  1235.8 94.6 %psum.124 = f32[]{:T(128)} all-reduce(f32[]{:T(128)} %get-tuple-element.14), channel_id=1, replica_groups=mesh['filt'=4,'il'=32,'xl'=4] {'filt','il','xl'}, use_global_device_ids=true, to_apply=%region_27.28 | all-reduce | flops 1 | bytes 8 | tf_op jit(solution)/shard_map/psum | solution.py:66
  1331.7 4.2 collective-permute-start.26
  1335.9 2.1 collective-permute-start.27
  1338.0 7.1 collective-permute-done.27
  1346.4 4.0 collective-permute-start.29
  1351.8 95.0 %psum.125 = f32[]{:T(128)} all-reduce(f32[]{:T(128)} %get-tuple-element.12), channel_id=1, replica_groups=mesh['filt'=4,'il'=32,'xl'=4] {'filt','il','xl'}, use_global_device_ids=true, to_apply=%region_29.30 | all-reduce | flops 1 | bytes 8 | tf_op jit(solution)/shard_map/psum | solution.py:101
  1448.8 94.2 %psum.126 = f32[]{:T(128)} all-reduce(f32[]{:T(128)} %get-tuple-element.10), channel_id=1, replica_groups=mesh['filt'=4,'il'=32,'xl'=4] {'filt','il','xl'}, use_global_device_ids=true, to_apply=%region_31.32 | all-reduce | flops 1 | bytes 8 | tf_op jit(solution)/shard_map/psum | solution.py:66
  1544.3 4.5 collective-permute-start.30
  1548.8 1.9 collective-permute-start.31
  1550.7 7.2 collective-permute-done.31
  1559.3 4.0 collective-permute-start.33
  1564.7 94.7 %psum.127 = f32[]{:T(128)} all-reduce(f32[]{:T(128)} %get-tuple-element.8), channel_id=1, replica_groups=mesh['filt'=4,'il'=32,'xl'=4] {'filt','il','xl'}, use_global_device_ids=true, to_apply=%region_33.34 | all-reduce | flops 1 | bytes 8 | tf_op jit(solution)/shard_map/psum | solution.py:101
  (101 shorter events, 28.2 us)
Async XLA Ops:
  1.5 15.9 collective-permute-start
  13.6 9.2 collective-permute-start.1
  31.6 2.9 copy-start.1
  34.9 2.9 copy-start
  38.2 0.9 copy-start.2
  39.2 9.9 copy-start.3
  49.1 15.4 collective-permute-start.2
  57.6 9.1 collective-permute-start.3
  60.8 11.2 all-to-all-start.1
  66.7 5.3 collective-permute-start.4
  68.0 4.8 collective-permute-start.5
  270.1 5.3 collective-permute-start.6
  273.4 9.1 collective-permute-start.7
  282.6 5.6 collective-permute-start.8
  283.9 5.1 collective-permute-start.9
  483.2 5.3 collective-permute-start.10
  486.6 9.1 collective-permute-start.11
  495.7 5.3 collective-permute-start.12
  497.0 4.8 collective-permute-start.13
  695.1 6.3 collective-permute-start.14
  699.4 9.1 collective-permute-start.15
  708.6 5.3 collective-permute-start.16
  709.9 4.8 collective-permute-start.17
  906.9 6.4 collective-permute-start.18
  911.4 9.1 collective-permute-start.19
  920.6 5.3 collective-permute-start.20
  921.9 4.8 collective-permute-start.21
  1119.2 6.5 collective-permute-start.22
  1123.8 9.1 collective-permute-start.23
  1132.9 5.3 collective-permute-start.24
  1134.2 4.8 collective-permute-start.25
  1331.7 6.3 collective-permute-start.26
  1335.9 9.1 collective-permute-start.27
  1345.1 5.3 collective-permute-start.28
  1346.4 4.8 collective-permute-start.29
  1544.3 6.4 collective-permute-start.30
  1548.8 9.1 collective-permute-start.31
  1558.0 5.3 collective-permute-start.32
  1559.3 4.8 collective-permute-start.33
where the time goes:
time: 1670 us; the launch traced here: 1660 us
  blocking collectives  1430 us (86%)
  starting transfers between devices  113 us (7%)
  waiting for transfers between devices  63.8 us (4%)
  between operations  21.4 us (1%)
  local copies, waits for them, and re-layouts  18.6 us (1%)
    psum x8, blocking collectives, squares(): return lax.psum(jnp.sum(residual * residual), ('filt', 'il', 'xl'))  760 us
    psum x7, blocking collectives, per_device(): lax.psum(jnp.sum(direction * image), ('filt', 'il', 'xl'))  663 us
    ppermute x17, starting transfers between devices, padded_2(): before = lax.ppermute(last, axis, up)  59.8 us
    ppermute x17, waiting for transfers between devices, padded_2(): before = lax.ppermute(last, axis, up)  58.4 us
    ppermute x17, starting transfers between devices, padded_2(): after = lax.ppermute(first, axis, down)  49.5 us
  transfers between devices with their start and end apart: 35, of which 17 were waited for; matrix products, arithmetic and copies ran while one was open for 0% of the time, Pallas kernels for 0%

commit v1 on v0

v1 whole, which is shorter than its diff:
```python
import jax
import jax.numpy as jnp
from jax import lax
from jax.experimental import pallas as pl
from jax.experimental.pallas import tpu as pltpu
from jax.sharding import Mesh, PartitionSpec as P

BAND = 8
KB = 2
HALF = 64
ITERS = 8
LANES = 128
SUB = 8

smooth_space = 4.0
smooth_time = 1.0
CENTRE = 19.0

GROUP = ("zh", "core", "zl")
PLANE = ("y", "x")
N_GROUP = 16
N_PLANE = 32
TRACES = 3
DEPTH = 24
VMEM = pl.BlockSpec(memory_space=pltpu.VMEM)
SMEM = pl.BlockSpec(memory_space=pltpu.SMEM)
F32 = jnp.float32


def lane_ids():
    return lax.broadcasted_iota(jnp.int32, (SUB, LANES), 1)


def row_ids():
    return lax.broadcasted_iota(jnp.int32, (SUB, LANES), 0)


def roll(value, amount, axis):
    return pltpu.roll(value, amount, axis) if amount else value


def pack_inputs(base_ref, mon_ref, bands_ref, quality_ref, out_ref, extra_ref):
    zl = lax.axis_index("zl")
    quarter = lax.axis_index("zh") * 2 + lax.axis_index("core")
    for group in range(N_GROUP):
        offset = ((zl - group % 4 + 1) & 3) - 1
        source = jnp.clip(group + offset, 0, N_GROUP - 1) >> 2
        out_ref[group, 0:16, :] = base_ref[source, 0]
        out_ref[group, 16:32, :] = mon_ref[source, 0]
    extra_ref[0:16, :] = quality_ref[0, 0]
    rows = lax.broadcasted_iota(jnp.int32, (SUB, 512), 0)
    bands = jnp.zeros((SUB, 512), F32)
    for block in range(2):
        for slot in range(KB):
            band = bands_ref[quarter, 0, block, slot].astype(F32)
            bands = jnp.where(rows == block * KB + slot, band, bands)
    extra_ref[16:24, :] = bands


def block_terms(base, padded, bands, lane):
    weight = jnp.zeros(base.shape, F32)
    moment = jnp.zeros(base.shape, F32)
    for band in bands:
        like_sum = jnp.zeros(base.shape, F32)
        step_sum = jnp.zeros(base.shape, F32)
        for quad in range(BAND // 4):
            terms = []
            for step in range(quad * 4, quad * 4 + 4):
                start = band * BAND + step
                turned = pltpu.roll(padded, (LANES - start) & (LANES - 1), 1)
                window = jnp.where(lane < LANES - start, turned[0:32], turned[8:40])
                difference = base - window
                misfit = (difference * difference).astype(jnp.bfloat16)
                terms.append(1.0 + misfit.astype(F32))
            a, b, c, d = terms
            left, right = a * b, c * d
            inverse = pl.reciprocal(left * right, approx=False)
            first, second = right * inverse, left * inverse
            low, high = (a + b) * first, (c + d) * second
            like_sum += low + high
            step_sum += a * first + c * second + 2.0 * high
            if quad:
                step_sum += (4.0 * quad) * (low + high)
        lag = (band * BAND - HALF).astype(F32)
        weight += like_sum
        moment += (lag * like_sum + step_sum) * (1.0 / HALF)
    scale = 1.0 / (KB * BAND)
    return weight * scale, moment * scale


def make_fields(recv_ref, below_ref, own_ref, above_ref, out_ref, target_ref):
    zl = lax.axis_index("zl")
    lane32 = lax.broadcasted_iota(jnp.int32, (32, LANES), 1)
    lane = lane_ids()
    for trace, extra_ref in enumerate((below_ref, own_ref, above_ref)):
        slot0 = (zl + trace - 1) & 3
        fields = []
        for block in range(2):
            rows = slice(block * 8, block * 8 + 8)
            mon_rows = slice(16 + block * 8, 24 + block * 8)
            base = jnp.concatenate([recv_ref[4 * c + slot0, rows, :] for c in range(4)], axis=0)
            mon = [recv_ref[4 * c + slot0, mon_rows, :] for c in range(4)]
            turned = [roll(v, 64, 1) for v in mon]
            zero = jnp.zeros((SUB, LANES), F32)
            sides = [zero] + turned + [zero]
            padded = jnp.concatenate(
                [jnp.where(lane < 64, sides[i], sides[i + 1]) for i in range(5)], axis=0
            )
            bands = [
                jnp.max(extra_ref[16 + block * KB + s : 17 + block * KB + s, 0:LANES]).astype(jnp.int32)
                for s in range(KB)
            ]
            weight, moment = block_terms(base, padded, bands, lane32)
            quality = jnp.concatenate(
                [extra_ref[rows, c * LANES : (c + 1) * LANES] for c in range(4)], axis=0
            )
            weight, moment = weight * quality, moment * quality
            if trace == 1:
                target_ref[block] = moment
            fields.append((weight, moment))
        padded_fields = []
        for f in range(2):
            for h in range(2):
                value = fields[h][f]
                turned = [roll(value[c * 8 : c * 8 + 8], 8, 1) for c in range(4)]
                sides = [zero] + turned + [zero]
                padded_fields.append([jnp.where(lane < 8, sides[i], sides[i + 1]) for i in range(5)])
        for piece in range(N_PLANE):
            part, offset = piece // 8, 16 * (piece % 8)
            packed = None
            for g, vregs in enumerate(padded_fields):
                shift = (32 * g - offset) % LANES
                value = roll(vregs[part], shift, 1)
                if piece % 8 == 7:
                    value = jnp.where(lane < 32 * g + 16, value, roll(vregs[part + 1], shift, 1))
                packed = value if packed is None else jnp.where(lane < 32 * g, packed, value)
            out_ref[piece, trace * 8 : trace * 8 + 8, :] = packed


def beside(values, lane, row):
    low, high = values
    next_low, next_high = roll(low, 7, 1), roll(high, 7, 1)
    turn_low, turn_high = roll(next_low, 96, 2), roll(next_high, 96, 2)
    last = row == 7
    up_low = jnp.where(last, jnp.where(lane < 96, turn_low, turn_high), next_low)
    up_high = jnp.where(last, jnp.where(lane < 96, turn_high, 0.0), next_high)
    prev_low, prev_high = roll(low, 1, 1), roll(high, 1, 1)
    turn_low, turn_high = roll(prev_low, 32, 2), roll(prev_high, 32, 2)
    first = row == 0
    down_low = jnp.where(first, jnp.where(lane < 32, 0.0, turn_low), prev_low)
    down_high = jnp.where(first, jnp.where(lane < 32, turn_low, turn_high), prev_high)
    return up_low + down_low, up_high + down_high


CHUNK = 2


def powers(recv_ref, out_ref, diag_ref, basis_ref):
    group = lax.axis_index("zh") * 8 + lax.axis_index("core") * 4 + lax.axis_index("zl")
    slab = lax.axis_index("y") * 4 + lax.axis_index("x")
    lane, row = lane_ids(), row_ids()
    tau = lane & 31
    time = slab * 16 - 8 + tau
    inside = ((time >= 0) & (time < 512)).astype(F32)
    shares = [
        inside * (group > 0).astype(F32),
        inside,
        inside * (group < N_GROUP - 1).astype(F32),
    ]
    space = [share * (2.0 * smooth_space / CENTRE) for share in shares]
    along = [share * (2.0 * smooth_time / CENTRE) for share in shares]
    for inline in range(DEPTH):
        trace, y = inline // 8, inline % 8
        for v in range(2):
            even = recv_ref[y * 4 + 2 * v, trace * 8 : trace * 8 + 8, :]
            odd = recv_ref[y * 4 + 2 * v + 1, trace * 8 : trace * 8 + 8, :]
            weight = jnp.where(lane < 64, even, roll(odd, 64, 1))
            target = jnp.where(lane < 64, roll(even, 64, 1), odd)
            centre = weight + (4.0 * smooth_space + 2.0 * smooth_time - CENTRE)
            diag_ref[v, inline] = centre * (shares[trace] * (2.0 / CENTRE))
            basis_ref[0, v, inline] = target
    lane3 = lax.broadcasted_iota(jnp.int32, (CHUNK, SUB, LANES), 2)
    row3 = lax.broadcasted_iota(jnp.int32, (CHUNK, SUB, LANES), 1)
    own = (tau >= 8) & (tau < 24)
    tile = jnp.zeros((SUB, LANES), F32)
    for level in range(ITERS):
        square = jnp.zeros((CHUNK, SUB, LANES), F32)
        cross = jnp.zeros((CHUNK, SUB, LANES), F32)
        begin = level + 1 + ((level + 1) % CHUNK and -1)
        for inline in range(begin, DEPTH - begin, CHUNK):
            region = inline // 8
            here = slice(inline, inline + CHUNK)
            centre = [basis_ref[level, v, here] for v in range(2)]
            sides = beside(centre, lane3, row3)
            for v in range(2):
                if inline == 0:
                    inlines = jnp.concatenate([jnp.zeros((1, SUB, LANES), F32), basis_ref[level, v, 0 : CHUNK - 1]], axis=0)
                else:
                    inlines = basis_ref[level, v, inline - 1 : inline - 1 + CHUNK]
                if inline + CHUNK == DEPTH:
                    inlines = inlines + jnp.concatenate(
                        [basis_ref[level, v, inline + 1 : DEPTH], jnp.zeros((1, SUB, LANES), F32)], axis=0
                    )
                else:
                    inlines = inlines + basis_ref[level, v, inline + 1 : inline + 1 + CHUNK]
                times = roll(centre[v], 1, 2) + roll(centre[v], LANES - 1, 2)
                image = (
                    diag_ref[v, here] * centre[v]
                    - space[region] * (inlines + sides[v])
                    - along[region] * times
                )
                image = 0.5 * image if level == 0 else image - basis_ref[level - 1, v, here]
                basis_ref[level + 1, v, here] = image
                if region == 1:
                    square += centre[v] * centre[v]
                    cross += centre[v] * image
        sums = []
        for value in (square, cross):
            value = jnp.where(own, jnp.sum(value, axis=0), 0.0)
            for shift in (4, 2, 1):
                value = value + roll(value, shift, 0)
            sums.append(value + roll(value, 64, 1))
        tile = jnp.where(row == level, jnp.where(lane < 64, sums[0], sums[1]), tile)
    for y in range(8):
        for v in range(2):
            pairs = []
            for k in range(1, 9, 2):
                pairs.append(
                    jnp.where(
                        tau < 16,
                        roll(basis_ref[k, v, 8 + y], 120, 1),
                        roll(basis_ref[k + 1, v, 8 + y], 8, 1),
                    )
                )
            turned = [roll(pair, 64, 1) for pair in pairs]
            for half in range(2):
                low, high = (pairs, turned) if half == 0 else (turned, pairs)
                piece = y * 4 + 2 * v + half
                for part in range(2):
                    out_ref[piece, part * 8 : part * 8 + 8, :] = jnp.where(
                        lane < 64, low[2 * part], high[2 * part + 1]
                    )
                out_ref[piece, 16:24, :] = tile


def spread_sums(recv_ref, out_ref):
    total = recv_ref[0, 16:24, :]
    for piece in range(1, N_PLANE):
        total = total + recv_ref[piece, 16:24, :]
    for group in range(N_GROUP):
        out_ref[group] = total


def operate_moments(moments, count):
    half = 0.5 * CENTRE
    return [CENTRE * moments[k] + half * (moments[k + 1] + moments[abs(k - 1)]) for k in range(count)]


def operate_terms(terms):
    half = 0.5 * CENTRE
    count = len(terms)
    out = []
    for k in range(count + 1):
        value = CENTRE * terms[k] if k < count else None
        if k >= 1:
            add = (CENTRE if k == 1 else half) * terms[k - 1]
            value = add if value is None else value + add
        if k + 1 < count:
            value = value + half * terms[k + 1]
        out.append(value)
    return out


def solve(squares, crosses):
    zero = jnp.zeros_like(squares[0])
    one = jnp.ones_like(squares[0])
    moments = [squares[0], crosses[0]]
    for k in range(1, ITERS):
        moments += [2.0 * squares[k] - squares[0], 2.0 * crosses[k] - crosses[0]]
    residual_m, direction_m = moments, moments
    residual, direction, shift = [one], [one], []
    norm = moments[0]
    for iteration in range(ITERS):
        count = 2 * ITERS - 1 - iteration
        image_m = operate_moments(direction_m, count)
        image = operate_terms(direction)
        bend = sum(direction[k] * image_m[k] for k in range(len(direction)))
        alpha = norm / bend
        shift = [
            alpha * direction[k] + (shift[k] if k < len(shift) else zero) for k in range(len(direction))
        ]
        residual = [
            (residual[k] if k < len(residual) else zero) - alpha * image[k] for k in range(len(image))
        ]
        if iteration + 1 < ITERS:
            residual_m = [residual_m[k] - alpha * image_m[k] for k in range(count)]
            after = sum(residual[k] * residual_m[k] for k in range(len(residual)))
            beta = after / norm
            direction = [
                residual[k] + (beta * direction[k] if k < len(direction) else zero)
                for k in range(len(residual))
            ]
            direction_m = [residual_m[k] + beta * direction_m[k] for k in range(count)]
            norm = after
    return shift, residual


def combine(basis_ref, sums_ref, target_ref, shift_ref, residual_ref):
    lane = lane_ids()
    total = sums_ref[0]
    for group in range(1, N_GROUP):
        total = total + sums_ref[group]
    left = jnp.where(lane < 64, total, 0.0)
    right = total - left
    for amount in (64, 32, 16, 8, 4, 2, 1):
        left = left + roll(left, amount, 1)
        right = right + roll(right, amount, 1)
    squares = [jnp.broadcast_to(left[k : k + 1], (SUB, LANES)) for k in range(ITERS)]
    crosses = [jnp.broadcast_to(right[k : k + 1], (SUB, LANES)) for k in range(ITERS)]
    shift, residual = solve(squares, crosses)
    shift = shift + [jnp.zeros_like(lane, F32)]
    first = (lane & 31) < 16
    for terms, out_ref in ((shift, shift_ref), (residual, residual_ref)):
        scale = [
            jnp.where(
                lane < 64,
                jnp.where(first, terms[k], terms[k + 1]),
                jnp.where(first, terms[k + 2], terms[k + 3]),
            )
            for k in (1, 5)
        ]
        for part in range(4):
            packed = [None, None]
            for step in range(8):
                piece = part * 8 + step
                value = scale[0] * basis_ref[piece, 0:8, :] + scale[1] * basis_ref[piece, 8:16, :]
                value = value + roll(value, 64, 1)
                value = value + roll(value, 112, 1)
                for h in range(2):
                    turned = roll(value, (16 * step - 32 * h) % LANES, 1)
                    packed[h] = turned if step == 0 else jnp.where(lane < 16 * step, packed[h], turned)
            for h in range(2):
                out_ref[0, 0, h * 8 : h * 8 + 8, part * LANES : (part + 1) * LANES] = (
                    packed[h] + terms[0] * target_ref[h, part * 8 : part * 8 + 8, :]
                )


def arrays(*shapes):
    return [jax.ShapeDtypeStruct(shape, F32) for shape in shapes]


def per_device(baseline, monitor, band_ids, quality):
    pieces, extra = pl.pallas_call(
        pack_inputs,
        out_shape=arrays((N_GROUP, 32, LANES), (DEPTH, 512)),
        in_specs=[VMEM, VMEM, SMEM, VMEM],
        name="pack_inputs",
    )(baseline, monitor, band_ids, quality)
    below = lax.ppermute(extra, GROUP, [(i, i + 1) for i in range(N_GROUP - 1)])
    above = lax.ppermute(extra, GROUP, [(i + 1, i) for i in range(N_GROUP - 1)])
    pieces = lax.all_to_all(pieces, GROUP, 0, 0, tiled=True)
    pieces, target = pl.pallas_call(
        make_fields,
        out_shape=arrays((N_PLANE, 8 * TRACES, LANES), (2, 32, LANES)),
        name="make_fields",
    )(pieces, below, extra, above)
    pieces = lax.all_to_all(pieces, PLANE, 0, 0, tiled=True)
    (pieces,) = pl.pallas_call(
        powers,
        out_shape=arrays((N_PLANE, 24, LANES)),
        scratch_shapes=[
            pltpu.VMEM((2, DEPTH, SUB, LANES), F32),
            pltpu.VMEM((ITERS + 1, 2, DEPTH, SUB, LANES), F32),
        ],
        name="powers",
    )(pieces)
    pieces = lax.all_to_all(pieces, PLANE, 0, 0, tiled=True)
    (sums,) = pl.pallas_call(
        spread_sums, out_shape=arrays((N_GROUP, SUB, LANES)), name="spread_sums"
    )(pieces)
    sums = lax.all_to_all(sums, GROUP, 0, 0, tiled=True)
    return tuple(
        pl.pallas_call(
            combine,
            out_shape=arrays((1, 1, 16, 512), (1, 1, 16, 512)),
            name="combine",
        )(pieces, sums, target)
    )


def solution(mesh):
    fine = Mesh(mesh.devices.reshape(2, 2, 4, 8, 4), ("zh", "core", "zl", "y", "x"))
    filt, il, xl = ("zh", "core"), ("zl", "y"), "x"
    split = P(filt, il, xl, None)
    in_specs = (P(None, il, xl, filt), P(None, il, xl, filt), P(None, il, xl, None), split)
    return jax.shard_map(
        per_device, mesh=fine, in_specs=in_specs, out_specs=(split, split), check_vma=False
    )
```

time: 1670 us -> 100 us (0.06)
  blocking collectives: 1430 us -> 57.5 us
  starting transfers between devices: 113 us -> 19.2 us
  waiting for transfers between devices: 63.8 us -> 5.28 us
  between operations: 21.4 us -> 0.66 us
    psum x15 -> x0, blocking collectives: 1420 us -> none  [the longest x8 760 us: squares(): return lax.psum(jnp.sum(residual * residual), ('filt', 'il', 'xl'))]
    ppermute x34 -> x2, starting transfers between devices: 109 us -> 7.26 us  [the longest x1 5.34 us: per_device(): above = lax.ppermute(extra, GROUP, [(i + 1, i) for i in range(N_GROUP - 1)])]
    ppermute x34 -> x2, waiting for transfers between devices: 63.8 us -> 5.28 us  [the longest x1 3.56 us: per_device(): below = lax.ppermute(extra, GROUP, [(i, i + 1) for i in range(N_GROUP - 1)])]
    all_to_all x1 -> x3, blocking collectives: 8.86 us -> 57.5 us  [the longest x2 42.9 us: per_device(): pieces = lax.all_to_all(pieces, PLANE, 0, 0, tiled=True)]
  transfers between devices with their start and end apart: 35 -> 3, of which waited for: 17 -> 2; matrix products, arithmetic and copies ran while one was open for 0% -> 0% of each run, Pallas kernels for 0% -> 0%
where the time goes in v1:
time: 100 us; the launch traced here: 99.5 us
  blocking collectives  57.5 us (58%)
  starting transfers between devices  19.2 us (19%)
  Pallas kernels  14.2 us (14%)
  waiting for transfers between devices  5.28 us (5%)
  local copies, waits for them, and re-layouts  2.66 us (3%)
    all_to_all x2, blocking collectives, per_device(): pieces = lax.all_to_all(pieces, PLANE, 0, 0, tiled=True)  42.9 us
    all_to_all x1, blocking collectives, per_device(): sums = lax.all_to_all(sums, GROUP, 0, 0, tiled=True)  14.6 us
    all_to_all x1, starting transfers between devices, per_device(): pieces = lax.all_to_all(pieces, GROUP, 0, 0, tiled=True)  12 us
    ppermute x1, starting transfers between devices, per_device(): above = lax.ppermute(extra, GROUP, [(i + 1, i) for i in range(N_GROUP - 1)])  5.34 us
    pallas_call x1, Pallas kernels, per_device(): pl.pallas_call(powers, out_shape=arrays((N_PLANE, 24, LANES)), scratch_sh...  4.27 us
    pallas_call x1, Pallas kernels, per_device(): pl.pallas_call(make_fields, out_shape=arrays((N_PLANE, 8 * TRACES, LANES)...  3.92 us
    ppermute x1, waiting for transfers between devices, per_device(): below = lax.ppermute(extra, GROUP, [(i, i + 1) for i in range(N_GROUP - 1)])  3.56 us
    pallas_call x1, Pallas kernels, per_device(): pl.pallas_call(combine, out_shape=arrays((1, 1, 16, 512), (1, 1, 16, 512)...  2.75 us
  transfers between devices with their start and end apart: 3, of which 2 were waited for; matrix products, arithmetic and copies ran while one was open for 0% of the time, Pallas kernels for 0%

profile of v1, /device:TPU:1, one launch (start us, length us, event | category | flops | bytes accessed | tf_op | source)
XLA Modules:
  0.0 99.5 jit_solution(12413393759999823238)
XLA Ops:
  0.6 1.4 %copy.6.bands_ref = s32[4,1,2,2]{3,2,1,0:T(2,128)} copy(s32[4,1,2,2]{0,3,2,1:T(2,128)} %param.6) | data formatting | bytes 128 | tf_op args[2]
  2.0 1.6 %pack_inputs.1 = (f32[16,32,128]{2,1,0:T(8,128)}, f32[24,512]{1,0:T(8,128)}) custom-call(f32[4,1,16,128]{3,2,1,0:T(8,128)} %base_ref.1, f32[4,1,16,128]{3,2,1,0:T(8,128)} %mon_ref.1, s32[4,1,2,2]{3,2,1,0:T(2,128)} %copy.6.bands_ref, f32[1,1,16,512]{3,2,1,0:T(8,128)} %quality_ref.1), custom_call_target="tpu_custom_call" | custom-call | tf_op jit(solution)/shard_map/pack_inputs/pallas_call | solution.py:353
  3.6 0.0 copy-start.1
  3.6 12.0 %all-to-all-start = ((f32[16,32,128]{2,1,0:T(8,128)}), f32[16,32,128]{2,1,0:T(8,128)S(1)}, u32[]{:S(2)}, u32[]{:S(2)}) async-start(f32[16,32,128]{2,1,0:T(8,128)} %get-tuple-element.6), calls=%async_computation | async-start | bytes 524288 | tf_op jit(solution)/shard_map/all_to_all | solution.py:361
  15.6 0.0 copy-done.1
  15.6 5.3 %collective-permute-start.1 = (f32[24,512]{1,0:T(8,128)S(1)}, f32[24,512]{1,0:T(8,128)S(1)}, u32[]{:S(2)}, u32[]{:S(2)}) collective-permute-start(f32[24,512]{1,0:T(8,128)S(1)} %copy-done.1), channel_id=1, source_target_pairs={{32,0},{64,32},{96,64},{128,96},{160,128},{192,160},{224,192},{256... | collective-permute-start | bytes 147464 | tf_op jit(solution)/shard_map/ppermute | solution.py:360
  20.9 1.9 %collective-permute-start = (f32[24,512]{1,0:T(8,128)S(1)}, f32[24,512]{1,0:T(8,128)S(1)}, u32[]{:S(2)}, u32[]{:S(2)}) collective-permute-start(f32[24,512]{1,0:T(8,128)S(1)} %copy-done.1), channel_id=1, source_target_pairs={{0,32},{32,64},{64,96},{96,128},{128,160},{160,192},{192,224},{224... | collective-permute-start | bytes 147464 | tf_op jit(solution)/shard_map/ppermute | solution.py:359
  22.8 1.7 %collective-permute-done.1.above_ref = f32[24,512]{1,0:T(8,128)S(1)} collective-permute-done((f32[24,512]{1,0:T(8,128)S(1)}, f32[24,512]{1,0:T(8,128)S(1)}, u32[]{:S(2)}, u32[]{:S(2)}) %collective-permute-start.1) | collective-permute-done | bytes 49184 | tf_op jit(solution)/shard_map/ppermute | solution.py:360
  24.6 0.0 copy-start.2
  24.6 3.6 %collective-permute-done.below_ref = f32[24,512]{1,0:T(8,128)S(1)} collective-permute-done((f32[24,512]{1,0:T(8,128)S(1)}, f32[24,512]{1,0:T(8,128)S(1)}, u32[]{:S(2)}, u32[]{:S(2)}) %collective-permute-start) | collective-permute-done | bytes 49184 | tf_op jit(solution)/shard_map/ppermute | solution.py:359
  28.1 0.0 copy-start.3
  28.1 0.0 all-to-all-done.recv_ref
  28.1 0.0 copy-done.2
  28.1 0.6 copy-done.3
  28.7 0.0 copy-start
  28.7 0.7 copy-done
  29.4 3.9 %make_fields.1 = (f32[32,24,128]{2,1,0:T(8,128)}, f32[2,32,128]{2,1,0:T(8,128)}) custom-call(f32[16,32,128]{2,1,0:T(8,128)} %copy-done, f32[24,512]{1,0:T(8,128)} %copy-done.3, f32[24,512]{1,0:T(8,128)} %get-tuple-element.7.own_ref, f32[24,512]{1,0:T(8,128)} %copy-done.2), custom_call_target="tpu_custom_call" | custom-call | tf_op jit(solution)/shard_map/make_fields/pallas_call | solution.py:362
  33.3 23.6 %all_to_all.20.recv_ref = f32[32,24,128]{2,1,0:T(8,128)} all-to-all(f32[32,24,128]{2,1,0:T(8,128)} %get-tuple-element.8), channel_id=1, replica_groups=mesh['zh'=2,'core'=2,'zl'=4,'y'=8,'x'=4] {'y','x'}, dimensions={0} | all-to-all | bytes 786432 | tf_op jit(solution)/shard_map/all_to_all | solution.py:367
  56.9 4.3 %powers.1 = f32[32,24,128]{2,1,0:T(8,128)} custom-call(f32[32,24,128]{2,1,0:T(8,128)} %all_to_all.20.recv_ref), custom_call_target="tpu_custom_call" | custom-call | tf_op jit(solution)/shard_map/powers/pallas_call | solution.py:368
  61.2 19.3 %all_to_all.21.recv_ref.basis_ref = f32[32,24,128]{2,1,0:T(8,128)} all-to-all(f32[32,24,128]{2,1,0:T(8,128)} %powers.1), channel_id=1, replica_groups=mesh['zh'=2,'core'=2,'zl'=4,'y'=8,'x'=4] {'y','x'}, dimensions={0} | all-to-all | bytes 786432 | tf_op jit(solution)/shard_map/all_to_all | solution.py:377
  80.5 1.6 %spread_sums.1 = f32[16,8,128]{2,1,0:T(8,128)} custom-call(f32[32,24,128]{2,1,0:T(8,128)} %all_to_all.21.recv_ref.basis_ref), custom_call_target="tpu_custom_call" | custom-call | tf_op jit(solution)/shard_map/spread_sums/pallas_call | solution.py:378
  82.2 14.6 %all_to_all.22.sums_ref = f32[16,8,128]{2,1,0:T(8,128)} all-to-all(f32[16,8,128]{2,1,0:T(8,128)} %spread_sums.1), channel_id=1, replica_groups=mesh['zh'=2,'core'=2,'zl'=4,'y'=8,'x'=4] {'zh','core','zl'}, dimensions={0} | all-to-all | bytes 131072 | tf_op jit(solution)/shard_map/all_to_all | solution.py:381
  96.7 2.7 %combine.1 = (f32[1,1,16,512]{3,2,1,0:T(8,128)}, f32[1,1,16,512]{3,2,1,0:T(8,128)}) custom-call(f32[32,24,128]{2,1,0:T(8,128)} %all_to_all.21.recv_ref.basis_ref, f32[16,8,128]{2,1,0:T(8,128)} %all_to_all.22.sums_ref, f32[2,32,128]{2,1,0:T(8,128)} %get-tuple-element.9.target_ref), custom_call_target="tpu_custom_call" | custom-call | tf_op jit(solution)/shard_map/combine/pallas_call | solution.py:383
Async XLA Ops:
  3.6 12.0 %copy-start.1 = (f32[24,512]{1,0:T(8,128)S(1)}, f32[24,512]{1,0:T(8,128)}, u32[]{:S(2)}) copy-start(f32[24,512]{1,0:T(8,128)} %get-tuple-element.7.own_ref) | copy-start | bytes 147460
  3.6 24.5 %all-to-all-start = ((f32[16,32,128]{2,1,0:T(8,128)}), f32[16,32,128]{2,1,0:T(8,128)S(1)}, u32[]{:S(2)}, u32[]{:S(2)}) async-start(f32[16,32,128]{2,1,0:T(8,128)} %get-tuple-element.6), calls=%async_computation | async-start | bytes 524288 | tf_op jit(solution)/shard_map/all_to_all | solution.py:361
  15.6 9.0 %collective-permute-start.1 = (f32[24,512]{1,0:T(8,128)S(1)}, f32[24,512]{1,0:T(8,128)S(1)}, u32[]{:S(2)}, u32[]{:S(2)}) collective-permute-start(f32[24,512]{1,0:T(8,128)S(1)} %copy-done.1), channel_id=1, source_target_pairs={{32,0},{64,32},{96,64},{128,96},{160,128},{192,160},{224,192},{256... | collective-permute-start | bytes 147464 | tf_op jit(solution)/shard_map/ppermute | solution.py:360
  20.9 7.2 %collective-permute-start = (f32[24,512]{1,0:T(8,128)S(1)}, f32[24,512]{1,0:T(8,128)S(1)}, u32[]{:S(2)}, u32[]{:S(2)}) collective-permute-start(f32[24,512]{1,0:T(8,128)S(1)} %copy-done.1), channel_id=1, source_target_pairs={{0,32},{32,64},{64,96},{96,128},{128,160},{160,192},{192,224},{224... | collective-permute-start | bytes 147464 | tf_op jit(solution)/shard_map/ppermute | solution.py:359
  24.6 3.6 %copy-start.2 = (f32[24,512]{1,0:T(8,128)}, f32[24,512]{1,0:T(8,128)S(1)}, u32[]{:S(2)}) copy-start(f32[24,512]{1,0:T(8,128)S(1)} %collective-permute-done.1.above_ref) | copy-start | bytes 147460
  28.1 0.6 copy-start.3
  28.7 0.7 copy-start

commit v2 on v1

--- a/solution.py
+++ b/solution.py
@@ -7,6 +7,7 @@
 
 BAND = 8
 KB = 2
+BXL = 8
 HALF = 64
 ITERS = 8
 LANES = 128
@@ -22,6 +23,9 @@
 N_PLANE = 32
 TRACES = 3
 DEPTH = 24
+FILT, IL = ("zh", "core"), ("zl", "y")
+LAGS = 128
+TRUST = 3e-4
 VMEM = pl.BlockSpec(memory_space=pltpu.VMEM)
 SMEM = pl.BlockSpec(memory_space=pltpu.SMEM)
 F32 = jnp.float32
@@ -52,7 +56,7 @@
     bands = jnp.zeros((SUB, 512), F32)
     for block in range(2):
         for slot in range(KB):
-            band = bands_ref[quarter, 0, block, slot].astype(F32)
+            band = bands_ref[0, block, slot, quarter].astype(F32)
             bands = jnp.where(rows == block * KB + slot, band, bands)
     extra_ref[16:24, :] = bands
 
@@ -251,89 +255,143 @@
         out_ref[group] = total
 
 
-def operate_moments(moments, count):
-    half = 0.5 * CENTRE
-    return [CENTRE * moments[k] + half * (moments[k + 1] + moments[abs(k - 1)]) for k in range(count)]
-
-
-def operate_terms(terms):
-    half = 0.5 * CENTRE
-    count = len(terms)
-    out = []
-    for k in range(count + 1):
-        value = CENTRE * terms[k] if k < count else None
-        if k >= 1:
-            add = (CENTRE if k == 1 else half) * terms[k - 1]
-            value = add if value is None else value + add
-        if k + 1 < count:
-            value = value + half * terms[k + 1]
-        out.append(value)
-    return out
-
-
-def solve(squares, crosses):
-    zero = jnp.zeros_like(squares[0])
-    one = jnp.ones_like(squares[0])
-    moments = [squares[0], crosses[0]]
-    for k in range(1, ITERS):
-        moments += [2.0 * squares[k] - squares[0], 2.0 * crosses[k] - crosses[0]]
-    residual_m, direction_m = moments, moments
-    residual, direction, shift = [one], [one], []
-    norm = moments[0]
-    for iteration in range(ITERS):
-        count = 2 * ITERS - 1 - iteration
-        image_m = operate_moments(direction_m, count)
-        image = operate_terms(direction)
-        bend = sum(direction[k] * image_m[k] for k in range(len(direction)))
-        alpha = norm / bend
-        shift = [
-            alpha * direction[k] + (shift[k] if k < len(shift) else zero) for k in range(len(direction))
-        ]
-        residual = [
-            (residual[k] if k < len(residual) else zero) - alpha * image[k] for k in range(len(image))
-        ]
-        if iteration + 1 < ITERS:
-            residual_m = [residual_m[k] - alpha * image_m[k] for k in range(count)]
-            after = sum(residual[k] * residual_m[k] for k in range(len(residual)))
-            beta = after / norm
-            direction = [
-                residual[k] + (beta * direction[k] if k < len(direction) else zero)
-                for k in range(len(residual))
-            ]
-            direction_m = [residual_m[k] + beta * direction_m[k] for k in range(count)]
-            norm = after
-    return shift, residual
-
-
-def combine(basis_ref, sums_ref, target_ref, shift_ref, residual_ref):
-    lane = lane_ids()
-    total = sums_ref[0]
+def two_sum(a, b):
+    total = a + b
+    part = total - a
+    return total, (a - (total - part)) + (b - part)
+
+
+def split(a):
+    scaled = 4097.0 * a
+    high = scaled - (scaled - a)
+    return high, a - high
+
+
+def across(tile, k):
+    return jnp.broadcast_to(tile[k : k + 1], (SUB, LANES))
+
+
+def lift(pair, turn):
+    return tuple(turn(part) for part in pair)
+
+
+def choose(mask, first, second):
+    return tuple(jnp.where(mask, a, b) for a, b in zip(first, second))
+
+
+def add_pairs(first, second):
+    total, error = two_sum(first[0], second[0])
+    return two_sum(total, error + (first[1] + second[1]))
+
+
+def solve(total, row, turn):
+    zero = jnp.zeros((SUB, LANES), F32)
+    fold = total
+    for amount in (96, 112, 120, 124, 126, 127):
+        fold = add_pairs(fold, lift(fold, lambda part: turn(part, amount, 1)))
+    squares = lift(fold, lambda part: jnp.broadcast_to(part[:, 0:1], (SUB, LANES)))
+    crosses = lift(fold, lambda part: jnp.broadcast_to(part[:, 64:65], (SUB, LANES)))
+    moments = [None] * (2 * ITERS)
+    for parity, pair in enumerate((squares, crosses)):
+        start = lift(pair, lambda part: across(part, 0))
+        doubled = add_pairs(lift(pair, lambda part: 2.0 * part), lift(start, lambda part: -part))
+        for k in range(ITERS):
+            moments[2 * k + parity] = lift(doubled, lambda part: across(part, k))
+
+    def column(values):
+        out = values[0]
+        for k in range(1, SUB):
+            out = choose(row < k, out, values[k])
+        return out
+
+    ahead, beyond, behind = column(moments[:8]), column(moments[8:]), column(moments[8:0:-1])
+    gram = []
+    for k in range(ITERS + 1):
+        later = choose(
+            row < 8 - k,
+            lift(ahead, lambda part: turn(part, (8 - k) % 8, 0)),
+            lift(beyond, lambda part: turn(part, (8 - k) % 8, 0)),
+        )
+        earlier = choose(
+            row < k,
+            lift(behind, lambda part: turn(part, k % 8, 0)),
+            lift(ahead, lambda part: turn(part, k % 8, 0)),
+        )
+        gram.append(add_pairs(later, earlier))
+    inverse = [gram[k][0] + 0.5 * (gram[k + 1][0] + gram[abs(k - 1)][0]) for k in range(ITERS)]
+    for k in range(ITERS):
+        reciprocal = 1.0 / across(inverse[k], k)
+        pivot = inverse[k]
+        for j in range(ITERS):
+            if j != k:
+                share = across(inverse[j], k) * reciprocal
+                inverse[j] = jnp.where(row == k, share, inverse[j] - pivot * share)
+        inverse[k] = jnp.where(row == k, reciprocal, -pivot * reciprocal)
+
+    def apply_inverse(right):
+        terms = [inverse[k] * across(right, k) for k in range(ITERS)]
+        while len(terms) > 1:
+            terms = [terms[k] + terms[k + 1] for k in range(0, len(terms), 2)]
+        return terms[0]
+
+    def remainder(series):
+        def lower(part):
+            return jnp.where(row == 0, 0.0, jnp.where(row == 1, 1.0, 0.5) * turn(part, 1, 0))
+
+        def upper(part):
+            return jnp.where(row == 7, 0.0, 0.5 * turn(part, 7, 0))
+
+        image = add_pairs(add_pairs(lift(series, lower), lift(series, upper)), series)
+        start = (jnp.where(row == 0, 1.0, 0.0), zero)
+        return add_pairs(start, lift(image, lambda part: -part)), lift(series, lambda part: -0.5 * across(part, 7))
+
+    parts = [split(pair[0]) for pair in gram]
+    series = (apply_inverse(gram[0][0]), zero)
+    steps = []
+    for _ in range(2):
+        body, top = remainder(series)
+        high, low = zero, zero
+        for k in range(ITERS + 1):
+            a, a_low = lift(body, lambda part: across(part, k)) if k < ITERS else top
+            b, b_low = gram[k]
+            (a0, a1), (b0, b1) = split(a), parts[k]
+            product = a * b
+            error = (((a0 * b0 - product) + a0 * b1) + a1 * b0) + a1 * b1
+            high, rest = two_sum(high, product)
+            low = low + (rest + (error + (a * b_low + a_low * b)))
+        change = apply_inverse(high + low)
+        steps.append(change)
+        series = two_sum(series[0], series[1] + change)
+    body, top = remainder(series)
+    return (series[0] + series[1]) * (1.0 / CENTRE), body[0] + body[1], top[0] + top[1], steps, series[0]
+
+
+def combine(basis_ref, sums_ref, target_ref, shift_ref, residual_ref, again_ref):
+    lane, row = lane_ids(), row_ids()
+    zero = jnp.zeros((SUB, LANES), F32)
+    total = (sums_ref[0], zero)
     for group in range(1, N_GROUP):
-        total = total + sums_ref[group]
-    left = jnp.where(lane < 64, total, 0.0)
-    right = total - left
-    for amount in (64, 32, 16, 8, 4, 2, 1):
-        left = left + roll(left, amount, 1)
-        right = right + roll(right, amount, 1)
-    squares = [jnp.broadcast_to(left[k : k + 1], (SUB, LANES)) for k in range(ITERS)]
-    crosses = [jnp.broadcast_to(right[k : k + 1], (SUB, LANES)) for k in range(ITERS)]
-    shift, residual = solve(squares, crosses)
-    shift = shift + [jnp.zeros_like(lane, F32)]
+        high, error = two_sum(total[0], sums_ref[group])
+        total = (high, total[1] + error)
+    shift, residual, last, steps, series = solve(total, row, roll)
+    fine = jnp.max(jnp.abs(steps[0])) <= TRUST * jnp.max(jnp.abs(series))
+    again_ref[0] = 1 - fine.astype(jnp.int32)
     first = (lane & 31) < 16
-    for terms, out_ref in ((shift, shift_ref), (residual, residual_ref)):
-        scale = [
+    for body, top, out_ref in ((shift, zero, shift_ref), (residual, last, residual_ref)):
+        terms = [across(body, k) for k in range(ITERS)] + [top]
+        low, high = (
             jnp.where(
                 lane < 64,
                 jnp.where(first, terms[k], terms[k + 1]),
                 jnp.where(first, terms[k + 2], terms[k + 3]),
             )
             for k in (1, 5)
-        ]
+        )
         for part in range(4):
             packed = [None, None]
             for step in range(8):
                 piece = part * 8 + step
-                value = scale[0] * basis_ref[piece, 0:8, :] + scale[1] * basis_ref[piece, 8:16, :]
+                value = low * basis_ref[piece, 0:8, :] + high * basis_ref[piece, 8:16, :]
                 value = value + roll(value, 64, 1)
                 value = value + roll(value, 112, 1)
                 for h in range(2):
@@ -345,8 +403,111 @@
                 )
 
 
+def limit(mebibytes):
+    return pltpu.CompilerParams(vmem_limit_bytes=mebibytes * 1024 * 1024)
+
+
 def arrays(*shapes):
     return [jax.ShapeDtypeStruct(shape, F32) for shape in shapes]
+
+
+def padded_2(value, sides, width):
+    for axis, dim in sides:
+        size, length = (lax.axis_size(axis), value.shape[dim])
+        up = [(i, (i + 1) % size) for i in range(size - 1)]
+        down = [(j, i) for i, j in up]
+        last = lax.slice_in_dim(value, length - width, length, axis=dim)
+        first = lax.slice_in_dim(value, 0, width, axis=dim)
+        before = lax.ppermute(last, axis, up)
+        after = lax.ppermute(first, axis, down)
+        value = jnp.concatenate([before, value, after], axis=dim)
+    return value
+
+
+def slot_window(block, band):
+    start = band * BAND
+    return lax.dynamic_slice(
+        block, (jnp.int32(0), start), (block.shape[0], block.shape[1] - LAGS + BAND)
+    )
+
+
+def lag_table(band_list):
+    steps = jnp.arange(BAND, dtype=jnp.float32)
+    return (band_list.astype(jnp.float32)[..., None] * BAND + steps - HALF) / HALF
+
+
+def moments(errors, lags):
+    likeness = 1.0 / (1.0 + errors.astype(jnp.float32))
+    weight_sum = jnp.sum(likeness, axis=(3, 4)) / (KB * BAND)
+    moment_sum = jnp.sum(lags[..., None, None] * likeness, axis=(3, 4)) / (KB * BAND)
+    return (weight_sum, moment_sum)
+
+
+def operate(field, weight):
+    padded = padded_2(field, ((FILT + IL, 0), ("x", 1)), 1)
+    centre = padded[1:-1, 1:-1, :]
+    across = (
+        4.0 * centre
+        - padded[2:, 1:-1, :]
+        - padded[:-2, 1:-1, :]
+        - padded[1:-1, 2:, :]
+        - padded[1:-1, :-2, :]
+    )
+    timed = jnp.pad(field, ((0, 0), (0, 0), (1, 1)))
+    along = 2.0 * field - timed[:, :, 2:] - timed[:, :, :-2]
+    return weight * field + smooth_space * across + smooth_time * along
+
+
+def squares(residual):
+    return lax.psum(jnp.sum(residual * residual), FILT + IL + ("x",))
+
+
+def step_by_step(baseline, monitor, band_ids, quality):
+    quarters, inline_rows, cross_rows, samples = baseline.shape
+    cross_blocks = cross_rows // BXL
+    extended = padded_2(monitor, ((FILT, 3),), HALF)
+    ext_blocks = extended.reshape(quarters, inline_rows, cross_blocks, BXL, samples + LAGS)
+    base_blocks = baseline.reshape(quarters, inline_rows, cross_blocks, BXL, samples)
+    per_slot = jax.vmap(slot_window, in_axes=(None, 0))
+    windows = jax.vmap(jax.vmap(jax.vmap(per_slot)))(ext_blocks, band_ids)
+    errors = jnp.stack(
+        [
+            jnp.square(
+                base_blocks[:, :, :, None] - windows[..., lag_step : lag_step + samples]
+            ).astype(jnp.bfloat16)
+            for lag_step in range(BAND)
+        ],
+        axis=4,
+    )
+    local_weight, local_moment = moments(errors, lag_table(band_ids))
+    weight_raw, moment_raw = (
+        lax.all_to_all(local_weight, FILT, split_axis=0, concat_axis=4, tiled=True),
+        lax.all_to_all(local_moment, FILT, split_axis=0, concat_axis=4, tiled=True),
+    )
+    total_time = weight_raw.shape[-1]
+    quality_grid = quality.reshape(inline_rows, cross_rows, total_time)
+    weight = quality_grid * weight_raw.reshape(inline_rows, cross_rows, total_time)
+    target = quality_grid * moment_raw.reshape(inline_rows, cross_rows, total_time)
+    shift = jnp.zeros_like(target)
+    residual = target
+    direction = target
+    norm_now = squares(residual)
+    for iteration in range(ITERS):
+        image = operate(direction, weight)
+        alpha = norm_now / lax.psum(jnp.sum(direction * image), FILT + IL + ("x",))
+        shift = shift + alpha * direction
+        residual = residual - alpha * image
+        norm_next = squares(residual)
+        direction = residual + norm_next / norm_now * direction
+        norm_now = norm_next
+    out_shape = (1, inline_rows, cross_rows, total_time)
+    return (shift.reshape(out_shape), residual.reshape(out_shape))
+
+
+def kernel(body, out_shape, mebibytes, **options):
+    return pl.pallas_call(
+        body, out_shape=out_shape, compiler_params=limit(mebibytes), name=body.__name__, **options
+    )
 
 
 def per_device(baseline, monitor, band_ids, quality):
@@ -355,44 +516,46 @@
         out_shape=arrays((N_GROUP, 32, LANES), (DEPTH, 512)),
         in_specs=[VMEM, VMEM, SMEM, VMEM],
         name="pack_inputs",
-    )(baseline, monitor, band_ids, quality)
+    )(baseline, monitor, band_ids.transpose(1, 2, 3, 0), quality)
     below = lax.ppermute(extra, GROUP, [(i, i + 1) for i in range(N_GROUP - 1)])
     above = lax.ppermute(extra, GROUP, [(i + 1, i) for i in range(N_GROUP - 1)])
     pieces = lax.all_to_all(pieces, GROUP, 0, 0, tiled=True)
-    pieces, target = pl.pallas_call(
-        make_fields,
-        out_shape=arrays((N_PLANE, 8 * TRACES, LANES), (2, 32, LANES)),
-        name="make_fields",
-    )(pieces, below, extra, above)
+    pieces, target = kernel(make_fields, arrays((N_PLANE, 8 * TRACES, LANES), (2, 32, LANES)), 8)(
+        pieces, below, extra, above
+    )
     pieces = lax.all_to_all(pieces, PLANE, 0, 0, tiled=True)
-    (pieces,) = pl.pallas_call(
+    (pieces,) = kernel(
         powers,
-        out_shape=arrays((N_PLANE, 24, LANES)),
+        arrays((N_PLANE, 24, LANES)),
+        8,
         scratch_shapes=[
             pltpu.VMEM((2, DEPTH, SUB, LANES), F32),
             pltpu.VMEM((ITERS + 1, 2, DEPTH, SUB, LANES), F32),
         ],
-        name="powers",
     )(pieces)
     pieces = lax.all_to_all(pieces, PLANE, 0, 0, tiled=True)
-    (sums,) = pl.pallas_call(
-        spread_sums, out_shape=arrays((N_GROUP, SUB, LANES)), name="spread_sums"
-    )(pieces)
+    (sums,) = kernel(spread_sums, arrays((N_GROUP, SUB, LANES)), 4)(pieces)
     sums = lax.all_to_all(sums, GROUP, 0, 0, tiled=True)
-    return tuple(
-        pl.pallas_call(
-            combine,
-            out_shape=arrays((1, 1, 16, 512), (1, 1, 16, 512)),
-            name="combine",
-        )(pieces, sums, target)
-    )
+    shift, residual, again = kernel(
+        combine,
+        arrays((1, 1, 16, 512), (1, 1, 16, 512)) + [jax.ShapeDtypeStruct((1,), jnp.int32)],
+        4,
+        out_specs=[VMEM, VMEM, SMEM],
+    )(pieces, sums, target)
+
+    def unsettled(state):
+        return state[2][0] != 0
+
+    def apart(state):
+        return step_by_step(baseline, monitor, band_ids, quality) + (jnp.zeros((1,), jnp.int32),)
+
+    return lax.while_loop(unsettled, apart, (shift, residual, again))[:2]
 
 
 def solution(mesh):
     fine = Mesh(mesh.devices.reshape(2, 2, 4, 8, 4), ("zh", "core", "zl", "y", "x"))
-    filt, il, xl = ("zh", "core"), ("zl", "y"), "x"
-    split = P(filt, il, xl, None)
-    in_specs = (P(None, il, xl, filt), P(None, il, xl, filt), P(None, il, xl, None), split)
+    outs = P(FILT, IL, "x", None)
+    in_specs = (P(None, IL, "x", FILT), P(None, IL, "x", FILT), P(None, IL, "x", None), outs)
     return jax.shard_map(
-        per_device, mesh=fine, in_specs=in_specs, out_specs=(split, split), check_vma=False
-    )
+        per_device, mesh=fine, in_specs=in_specs, out_specs=(outs, outs), check_vma=False
+    )

time: 100 us -> 91.1 us (0.911)
  Pallas kernels: 14.2 us -> 8.16 us
  waiting for transfers between devices: 5.28 us -> 2.65 us
  local copies, waits for them, and re-layouts: 2.66 us -> 0.82 us
    pallas_call x4, Pallas kernels: 12.6 us -> 6.58 us  [the longest x1 2.51 us: per_device(): kernel(powers, arrays((N_PLANE, 24, LANES)), 8, scratch_shapes=[pltpu.VME...]
    all_to_all x1, blocking collectives: 14.6 us -> 17 us  [per_device(): sums = lax.all_to_all(sums, GROUP, 0, 0, tiled=True)]
    unnamed x9 -> x8, local copies, waits for them, and re-layouts: 2.66 us -> 0.82 us
    all_to_all x2, blocking collectives: 42.9 us -> 41.1 us  [per_device(): pieces = lax.all_to_all(pieces, PLANE, 0, 0, tiled=True)]
    ppermute x1, waiting for transfers between devices: 3.56 us -> 1.79 us  [per_device(): below = lax.ppermute(extra, GROUP, [(i, i + 1) for i in range(N_GROUP - 1)])]
    ppermute x1, starting transfers between devices: 1.92 us -> 3.28 us  [per_device(): below = lax.ppermute(extra, GROUP, [(i, i + 1) for i in range(N_GROUP - 1)])]
    ppermute x1, starting transfers between devices: 5.34 us -> 4.07 us  [per_device(): above = lax.ppermute(extra, GROUP, [(i + 1, i) for i in range(N_GROUP - 1)])]
    ppermute x1, waiting for transfers between devices: 1.72 us -> 0.64 us  [per_device(): above = lax.ppermute(extra, GROUP, [(i + 1, i) for i in range(N_GROUP - 1)])]
  transfers between devices with their start and end apart: 3 -> 3, of which waited for: 2 -> 3; matrix products, arithmetic and copies ran while one was open for 0% -> 0% of each run, Pallas kernels for 0% -> 0%
where the time goes in v2:
time: 91.1 us; the launch traced here: 90.6 us
  blocking collectives  58.1 us (64%)
  starting transfers between devices  19.2 us (21%)
  Pallas kernels  8.16 us (9%)
  waiting for transfers between devices  2.65 us (3%)
    all_to_all x2, blocking collectives, per_device(): pieces = lax.all_to_all(pieces, PLANE, 0, 0, tiled=True)  41.1 us
    all_to_all x1, blocking collectives, per_device(): sums = lax.all_to_all(sums, GROUP, 0, 0, tiled=True)  17 us
    all_to_all x1, starting transfers between devices, per_device(): pieces = lax.all_to_all(pieces, GROUP, 0, 0, tiled=True)  11.8 us
    ppermute x1, starting transfers between devices, per_device(): above = lax.ppermute(extra, GROUP, [(i + 1, i) for i in range(N_GROUP - 1)])  4.07 us
    ppermute x1, starting transfers between devices, per_device(): below = lax.ppermute(extra, GROUP, [(i, i + 1) for i in range(N_GROUP - 1)])  3.28 us
    pallas_call x1, Pallas kernels, per_device(): kernel(powers, arrays((N_PLANE, 24, LANES)), 8, scratch_shapes=[pltpu.VME...  2.51 us
    pallas_call x1, Pallas kernels, per_device(): kernel(make_fields, arrays((N_PLANE, 8 * TRACES, LANES), (2, 32, LANES)), 8)  2.2 us
    pallas_call x1, Pallas kernels, per_device(): kernel(combine, arrays((1, 1, 16, 512), (1, 1, 16, 512)) + [jax.ShapeDtyp...  1.83 us
  transfers between devices with their start and end apart: 3, of which 3 were waited for; matrix products, arithmetic and copies ran while one was open for 0% of the time, Pallas kernels for 0%

profile of v2, /device:TPU:1, one launch (start us, length us, event | category | flops | bytes accessed | tf_op | source)
XLA Modules:
  0.0 90.6 jit_solution(1066921200128756774)
XLA Ops:
  0.6 1.6 %pack_inputs.1 = (f32[16,32,128]{2,1,0:T(8,128)}, f32[24,512]{1,0:T(8,128)}) custom-call(f32[4,1,16,128]{3,2,1,0:T(8,128)} %base_ref.1, f32[4,1,16,128]{3,2,1,0:T(8,128)} %mon_ref.1, s32[1,2,2,4]{3,2,1,0:T(2,128)} %bitcast.98, f32[1,1,16,512]{3,2,1,0:T(8,128)} %quality_ref.1), custom_call_target="tpu_custom_call" | custom-call | tf_op jit(solution)/shard_map/pack_inputs/pallas_call | solution.py:514
  2.2 11.8 %all-to-all-start.2 = ((f32[16,32,128]{2,1,0:T(8,128)}), f32[16,32,128]{2,1,0:T(8,128)S(1)}, u32[]{:S(2)}, u32[]{:S(2)}) async-start(f32[16,32,128]{2,1,0:T(8,128)} %get-tuple-element.44), calls=%async_computation.2 | async-start | bytes 524288 | tf_op jit(solution)/shard_map/all_to_all | solution.py:522
  14.0 3.3 %collective-permute-start.34 = (f32[24,512]{1,0:T(8,128)}, f32[24,512]{1,0:T(8,128)S(1)}, u32[]{:S(2)}, u32[]{:S(2)}) collective-permute-start(f32[24,512]{1,0:T(8,128)} %get-tuple-element.45.own_ref), channel_id=1, source_target_pairs={{0,32},{32,64},{64,96},{96,128},{128,160},{160,192},{192,224},{224... | collective-permute-start | bytes 147464 | tf_op jit(solution)/shard_map/ppermute | solution.py:520
  17.3 4.1 %collective-permute-start.35 = (f32[24,512]{1,0:T(8,128)}, f32[24,512]{1,0:T(8,128)S(1)}, u32[]{:S(2)}, u32[]{:S(2)}) collective-permute-start(f32[24,512]{1,0:T(8,128)} %get-tuple-element.45.own_ref), channel_id=1, source_target_pairs={{32,0},{64,32},{96,64},{128,96},{160,128},{192,160},{224,192},{256... | collective-permute-start | bytes 147464 | tf_op jit(solution)/shard_map/ppermute | solution.py:521
  21.4 1.8 %collective-permute-done.34.below_ref = f32[24,512]{1,0:T(8,128)S(1)} collective-permute-done((f32[24,512]{1,0:T(8,128)}, f32[24,512]{1,0:T(8,128)S(1)}, u32[]{:S(2)}, u32[]{:S(2)}) %collective-permute-start.34) | collective-permute-done | bytes 49184 | tf_op jit(solution)/shard_map/ppermute | solution.py:520
  23.2 0.6 collective-permute-done.35.above_ref
  23.8 0.2 all-to-all-done.2.recv_ref
  24.1 0.0 copy-start
  24.1 0.8 copy-done
  24.9 2.2 %make_fields.1 = (f32[32,24,128]{2,1,0:T(8,128)S(1)}, f32[2,32,128]{2,1,0:T(8,128)S(1)}) custom-call(f32[16,32,128]{2,1,0:T(8,128)S(1)} %all-to-all-done.2.recv_ref, f32[24,512]{1,0:T(8,128)S(1)} %collective-permute-done.34.below_ref, f32[24,512]{1,0:T(8,128)S(1)} %copy-done, f32[24,512]{1,0:T(8,128)S(1)} %collective-permute-done.35.above_ref), custom_call_target="tpu_custom_call" | custom-call | tf_op jit(solution)/shard_map/make_fields/pallas_call | solution.py:523
  27.1 23.4 %all_to_all.45.recv_ref = f32[32,24,128]{2,1,0:T(8,128)S(1)} all-to-all(f32[32,24,128]{2,1,0:T(8,128)S(1)} %get-tuple-element.46), channel_id=1, replica_groups=mesh['zh'=2,'core'=2,'zl'=4,'y'=8,'x'=4] {'y','x'}, dimensions={0} | all-to-all | bytes 786432 | tf_op jit(solution)/shard_map/all_to_all | solution.py:526
  50.4 2.5 %powers.1 = f32[32,24,128]{2,1,0:T(8,128)S(1)} custom-call(f32[32,24,128]{2,1,0:T(8,128)S(1)} %all_to_all.45.recv_ref), custom_call_target="tpu_custom_call" | custom-call | tf_op jit(solution)/shard_map/powers/pallas_call | solution.py:527
  53.0 0.0 copy-start.3
  53.0 0.0 copy-start.4
  53.0 0.0 copy-start.7
  53.0 17.7 %all_to_all.46.recv_ref.basis_ref = f32[32,24,128]{2,1,0:T(8,128)S(1)} all-to-all(f32[32,24,128]{2,1,0:T(8,128)S(1)} %powers.1), channel_id=1, replica_groups=mesh['zh'=2,'core'=2,'zl'=4,'y'=8,'x'=4] {'y','x'}, dimensions={0} | all-to-all | bytes 786432 | tf_op jit(solution)/shard_map/all_to_all | solution.py:536
  70.8 17.0 %all_to_all.47.sums_ref = f32[16,8,128]{2,1,0:T(8,128)S(1)} all-to-all(f32[16,8,128]{2,1,0:T(8,128)S(1)} %spread_sums.1), channel_id=1, replica_groups=mesh['zh'=2,'core'=2,'zl'=4,'y'=8,'x'=4] {'zh','core','zl'}, dimensions={0} | all-to-all | bytes 131072 | tf_op jit(solution)/shard_map/all_to_all | solution.py:538
  87.8 1.8 %combine.1 = (f32[1,1,16,512]{3,2,1,0:T(8,128)}, f32[1,1,16,512]{3,2,1,0:T(8,128)}, s32[1]{0:T(128)}) custom-call(f32[32,24,128]{2,1,0:T(8,128)S(1)} %all_to_all.46.recv_ref.basis_ref, f32[16,8,128]{2,1,0:T(8,128)S(1)} %all_to_all.47.sums_ref, f32[2,32,128]{2,1,0:T(8,128)S(1)} %get-tuple-element.47.target_ref), custom_call_target="tpu_custom_call" | custom-call | tf_op jit(solution)/shard_map/combine/pallas_call | solution.py:539
  89.6 0.0 copy-done.3
  89.6 0.0 copy-done.4
  89.6 0.0 copy-done.7
  89.6 0.8 while.11
  (1 shorter events, 0.0 us)
Async XLA Ops:
  2.2 21.9 %all-to-all-start.2 = ((f32[16,32,128]{2,1,0:T(8,128)}), f32[16,32,128]{2,1,0:T(8,128)S(1)}, u32[]{:S(2)}, u32[]{:S(2)}) async-start(f32[16,32,128]{2,1,0:T(8,128)} %get-tuple-element.44), calls=%async_computation.2 | async-start | bytes 524288 | tf_op jit(solution)/shard_map/all_to_all | solution.py:522
  14.0 9.1 %collective-permute-start.34 = (f32[24,512]{1,0:T(8,128)}, f32[24,512]{1,0:T(8,128)S(1)}, u32[]{:S(2)}, u32[]{:S(2)}) collective-permute-start(f32[24,512]{1,0:T(8,128)} %get-tuple-element.45.own_ref), channel_id=1, source_target_pairs={{0,32},{32,64},{64,96},{96,128},{128,160},{160,192},{192,224},{224... | collective-permute-start | bytes 147464 | tf_op jit(solution)/shard_map/ppermute | solution.py:520
  17.3 6.5 %collective-permute-start.35 = (f32[24,512]{1,0:T(8,128)}, f32[24,512]{1,0:T(8,128)S(1)}, u32[]{:S(2)}, u32[]{:S(2)}) collective-permute-start(f32[24,512]{1,0:T(8,128)} %get-tuple-element.45.own_ref), channel_id=1, source_target_pairs={{32,0},{64,32},{96,64},{128,96},{160,128},{192,160},{224,192},{256... | collective-permute-start | bytes 147464 | tf_op jit(solution)/shard_map/ppermute | solution.py:521
  24.1 0.8 copy-start
  53.0 36.7 %copy-start.3 = (f32[4,1,16,128]{3,2,1,0:T(8,128)S(1)}, f32[4,1,16,128]{3,2,1,0:T(8,128)}, u32[]{:S(2)}) copy-start(f32[4,1,16,128]{3,2,1,0:T(8,128)} %base_ref.1) | copy-start | bytes 98308
  53.0 36.7 %copy-start.4 = (f32[4,1,16,128]{3,2,1,0:T(8,128)S(1)}, f32[4,1,16,128]{3,2,1,0:T(8,128)}, u32[]{:S(2)}) copy-start(f32[4,1,16,128]{3,2,1,0:T(8,128)} %mon_ref.1) | copy-start | bytes 98308
  53.0 36.7 %copy-start.7 = (s32[4,1,2,2]{0,3,2,1:T(2,128)S(1)}, s32[4,1,2,2]{0,3,2,1:T(2,128)}, u32[]{:S(2)}) copy-start(s32[4,1,2,2]{0,3,2,1:T(2,128)} %param.8) | copy-start | bytes 196

commit v3 on v2

--- a/solution.py
+++ b/solution.py
@@ -21,7 +21,8 @@
 PLANE = ("y", "x")
 N_GROUP = 16
 N_PLANE = 32
-TRACES = 3
+ROWS = 17
+FIXED = 2.0**29
 DEPTH = 24
 FILT, IL = ("zh", "core"), ("zl", "y")
 LAGS = 128
@@ -92,20 +93,39 @@
     return weight * scale, moment * scale
 
 
+def spread(value, lane, zero):
+    turned = [roll(value[c * 8 : c * 8 + 8], 8, 1) for c in range(4)]
+    sides = [zero] + turned + [zero]
+    return [jnp.where(lane < 8, sides[i], sides[i + 1]) for i in range(5)]
+
+
+def code(weight, target):
+    high = (jnp.sqrt(weight * 0.5) * 65535.0 + 0.5).astype(jnp.int32)
+    low = (jnp.sqrt(jnp.sqrt(jnp.abs(target) * 0.5)) * 32767.0 + 0.5).astype(jnp.int32)
+    low = jnp.where(target < 0.0, -low, low)
+    return (high << 16) | (low & 65535)
+
+
+def decode(coded):
+    high = lax.shift_right_logical(coded, 16).astype(F32) * (2.0**0.5 / 65535.0)
+    low = ((coded << 16) >> 16).astype(F32) * (2.0**0.25 / 32767.0)
+    return high * high, low * jnp.abs(low) * (low * low)
+
+
 def make_fields(recv_ref, below_ref, own_ref, above_ref, out_ref, target_ref):
     zl = lax.axis_index("zl")
     lane32 = lax.broadcasted_iota(jnp.int32, (32, LANES), 1)
     lane = lane_ids()
+    zero = jnp.zeros((SUB, LANES), F32)
+    empty = jnp.zeros((SUB, LANES), jnp.int32)
+    exact, coded = [None] * 4, []
     for trace, extra_ref in enumerate((below_ref, own_ref, above_ref)):
         slot0 = (zl + trace - 1) & 3
-        fields = []
         for block in range(2):
             rows = slice(block * 8, block * 8 + 8)
             mon_rows = slice(16 + block * 8, 24 + block * 8)
             base = jnp.concatenate([recv_ref[4 * c + slot0, rows, :] for c in range(4)], axis=0)
-            mon = [recv_ref[4 * c + slot0, mon_rows, :] for c in range(4)]
-            turned = [roll(v, 64, 1) for v in mon]
-            zero = jnp.zeros((SUB, LANES), F32)
+            turned = [roll(recv_ref[4 * c + slot0, mon_rows, :], 64, 1) for c in range(4)]
             sides = [zero] + turned + [zero]
             padded = jnp.concatenate(
                 [jnp.where(lane < 64, sides[i], sides[i + 1]) for i in range(5)], axis=0
@@ -121,24 +141,21 @@
             weight, moment = weight * quality, moment * quality
             if trace == 1:
                 target_ref[block] = moment
-            fields.append((weight, moment))
-        padded_fields = []
-        for f in range(2):
-            for h in range(2):
-                value = fields[h][f]
-                turned = [roll(value[c * 8 : c * 8 + 8], 8, 1) for c in range(4)]
-                sides = [zero] + turned + [zero]
-                padded_fields.append([jnp.where(lane < 8, sides[i], sides[i + 1]) for i in range(5)])
+                exact[block] = spread((weight * FIXED).astype(jnp.int32), lane, empty)
+                exact[2 + block] = spread((moment * FIXED).astype(jnp.int32), lane, empty)
+            else:
+                coded.append(spread(code(weight, moment), lane, empty))
+    for at, fields in enumerate((exact, coded)):
         for piece in range(N_PLANE):
             part, offset = piece // 8, 16 * (piece % 8)
             packed = None
-            for g, vregs in enumerate(padded_fields):
+            for g, vregs in enumerate(fields):
                 shift = (32 * g - offset) % LANES
                 value = roll(vregs[part], shift, 1)
                 if piece % 8 == 7:
                     value = jnp.where(lane < 32 * g + 16, value, roll(vregs[part + 1], shift, 1))
                 packed = value if packed is None else jnp.where(lane < 32 * g, packed, value)
-            out_ref[piece, trace * 8 : trace * 8 + 8, :] = packed
+            out_ref[piece, at * 8 : at * 8 + 8, :] = packed
 
 
 def beside(values, lane, row):
@@ -173,20 +190,26 @@
     ]
     space = [share * (2.0 * smooth_space / CENTRE) for share in shares]
     along = [share * (2.0 * smooth_time / CENTRE) for share in shares]
-    for inline in range(DEPTH):
-        trace, y = inline // 8, inline % 8
+    def place(inline, weight, target):
+        centre = weight + (4.0 * smooth_space + 2.0 * smooth_time - CENTRE)
+        diag_ref[v, inline] = centre * (shares[inline // 8] * (2.0 / CENTRE))
+        basis_ref[0, v, inline] = target
+
+    for y in range(8):
         for v in range(2):
-            even = recv_ref[y * 4 + 2 * v, trace * 8 : trace * 8 + 8, :]
-            odd = recv_ref[y * 4 + 2 * v + 1, trace * 8 : trace * 8 + 8, :]
-            weight = jnp.where(lane < 64, even, roll(odd, 64, 1))
-            target = jnp.where(lane < 64, roll(even, 64, 1), odd)
-            centre = weight + (4.0 * smooth_space + 2.0 * smooth_time - CENTRE)
-            diag_ref[v, inline] = centre * (shares[trace] * (2.0 / CENTRE))
-            basis_ref[0, v, inline] = target
+            joined = []
+            for at in range(2):
+                even = recv_ref[y * 4 + 2 * v, at * 8 : at * 8 + 8, :]
+                odd = recv_ref[y * 4 + 2 * v + 1, at * 8 : at * 8 + 8, :]
+                joined.append(jnp.where(lane < 64, even, roll(odd, 64, 1)))
+                joined.append(jnp.where(lane < 64, roll(even, 64, 1), odd))
+            place(8 + y, joined[0].astype(F32) * (1.0 / FIXED), joined[1].astype(F32) * (1.0 / FIXED))
+            place(y, *decode(joined[2]))
+            place(16 + y, *decode(joined[3]))
     lane3 = lax.broadcasted_iota(jnp.int32, (CHUNK, SUB, LANES), 2)
     row3 = lax.broadcasted_iota(jnp.int32, (CHUNK, SUB, LANES), 1)
     own = (tau >= 8) & (tau < 24)
-    tile = jnp.zeros((SUB, LANES), F32)
+    squares, crosses = [], []
     for level in range(ITERS):
         square = jnp.zeros((CHUNK, SUB, LANES), F32)
         cross = jnp.zeros((CHUNK, SUB, LANES), F32)
@@ -218,13 +241,24 @@
                 if region == 1:
                     square += centre[v] * centre[v]
                     cross += centre[v] * image
-        sums = []
-        for value in (square, cross):
-            value = jnp.where(own, jnp.sum(value, axis=0), 0.0)
-            for shift in (4, 2, 1):
-                value = value + roll(value, shift, 0)
-            sums.append(value + roll(value, 64, 1))
-        tile = jnp.where(row == level, jnp.where(lane < 64, sums[0], sums[1]), tile)
+        squares.append(jnp.where(own, jnp.sum(square, axis=0), 0.0))
+        crosses.append(jnp.where(own, jnp.sum(cross, axis=0), 0.0))
+    tiles = []
+    for values in (squares, crosses):
+        for amount in (4, 2, 1):
+            values = [
+                jnp.where(
+                    (row & amount) == 0, a + roll(a, 8 - amount, 0), b + roll(b, amount, 0)
+                )
+                for a, b in zip(values[:amount], values[amount:])
+            ]
+        tile = values[0]
+        for amount in (64, 32, 16, 8):
+            tile = tile + roll(tile, amount, 1)
+        tiles.append(tile)
+    tile = jnp.where(((lane >> 3) & 7) == row, jnp.where(lane < 64, tiles[0], tiles[1]), 0.0)
+    for amount in (4, 2, 1):
+        tile = tile + roll(tile, amount, 0)
     for y in range(8):
         for v in range(2):
             pairs = []
@@ -241,18 +275,18 @@
                 low, high = (pairs, turned) if half == 0 else (turned, pairs)
                 piece = y * 4 + 2 * v + half
                 for part in range(2):
-                    out_ref[piece, part * 8 : part * 8 + 8, :] = jnp.where(
+                    at = piece * ROWS + part * 8
+                    out_ref[at : at + 8, :] = jnp.where(
                         lane < 64, low[2 * part], high[2 * part + 1]
                     )
-                out_ref[piece, 16:24, :] = tile
+                out_ref[piece * ROWS + 16 : piece * ROWS + 17, :] = tile[0:1]
 
 
 def spread_sums(recv_ref, out_ref):
-    total = recv_ref[0, 16:24, :]
-    for piece in range(1, N_PLANE):
-        total = total + recv_ref[piece, 16:24, :]
-    for group in range(N_GROUP):
-        out_ref[group] = total
+    terms = [recv_ref[piece * ROWS + 16 : piece * ROWS + 17, :] for piece in range(N_PLANE)]
+    while len(terms) > 1:
+        terms = [terms[k] + terms[k + 1] for k in range(0, len(terms), 2)]
+    out_ref[...] = jnp.broadcast_to(terms[0], (N_GROUP, LANES))
 
 
 def two_sum(a, b):
@@ -284,19 +318,20 @@
     return two_sum(total, error + (first[1] + second[1]))
 
 
-def solve(total, row, turn):
+def solve(total, lane, row, turn):
     zero = jnp.zeros((SUB, LANES), F32)
     fold = total
-    for amount in (96, 112, 120, 124, 126, 127):
+    for amount in (4, 2, 1):
+        fold = add_pairs(fold, lift(fold, lambda part: turn(part, amount, 0)))
+    for amount in (124, 126, 127):
         fold = add_pairs(fold, lift(fold, lambda part: turn(part, amount, 1)))
-    squares = lift(fold, lambda part: jnp.broadcast_to(part[:, 0:1], (SUB, LANES)))
-    crosses = lift(fold, lambda part: jnp.broadcast_to(part[:, 64:65], (SUB, LANES)))
-    moments = [None] * (2 * ITERS)
-    for parity, pair in enumerate((squares, crosses)):
-        start = lift(pair, lambda part: across(part, 0))
-        doubled = add_pairs(lift(pair, lambda part: 2.0 * part), lift(start, lambda part: -part))
-        for k in range(ITERS):
-            moments[2 * k + parity] = lift(doubled, lambda part: across(part, k))
+
+    def at_lane(pair, k):
+        return lift(pair, lambda part: jnp.broadcast_to(part[:, k : k + 1], (SUB, LANES)))
+
+    start = choose(lane < 64, at_lane(fold, 0), at_lane(fold, 64))
+    doubled = add_pairs(lift(fold, lambda part: 2.0 * part), lift(start, lambda part: -part))
+    moments = [at_lane(doubled, 64 * (k % 2) + 8 * (k // 2)) for k in range(2 * ITERS)]
 
     def column(values):
         out = values[0]
@@ -369,11 +404,8 @@
 def combine(basis_ref, sums_ref, target_ref, shift_ref, residual_ref, again_ref):
     lane, row = lane_ids(), row_ids()
     zero = jnp.zeros((SUB, LANES), F32)
-    total = (sums_ref[0], zero)
-    for group in range(1, N_GROUP):
-        high, error = two_sum(total[0], sums_ref[group])
-        total = (high, total[1] + error)
-    shift, residual, last, steps, series = solve(total, row, roll)
+    total = two_sum(sums_ref[0:8, :], sums_ref[8:16, :])
+    shift, residual, last, steps, series = solve(total, lane, row, roll)
     fine = jnp.max(jnp.abs(steps[0])) <= TRUST * jnp.max(jnp.abs(series))
     again_ref[0] = 1 - fine.astype(jnp.int32)
     first = (lane & 31) < 16
@@ -391,7 +423,8 @@
             packed = [None, None]
             for step in range(8):
                 piece = part * 8 + step
-                value = low * basis_ref[piece, 0:8, :] + high * basis_ref[piece, 8:16, :]
+                at = piece * ROWS
+                value = low * basis_ref[at : at + 8, :] + high * basis_ref[at + 8 : at + 16, :]
                 value = value + roll(value, 64, 1)
                 value = value + roll(value, 112, 1)
                 for h in range(2):
@@ -504,6 +537,11 @@
     return (shift.reshape(out_shape), residual.reshape(out_shape))
 
 
+def exchange(rows, axes, count):
+    pieces = lax.all_to_all(rows.reshape(-1, count, 1, LANES), axes, 0, 0, tiled=True)
+    return pieces.reshape(rows.shape)
+
+
 def kernel(body, out_shape, mebibytes, **options):
     return pl.pallas_call(
         body, out_shape=out_shape, compiler_params=limit(mebibytes), name=body.__name__, **options
@@ -520,22 +558,26 @@
     below = lax.ppermute(extra, GROUP, [(i, i + 1) for i in range(N_GROUP - 1)])
     above = lax.ppermute(extra, GROUP, [(i + 1, i) for i in range(N_GROUP - 1)])
     pieces = lax.all_to_all(pieces, GROUP, 0, 0, tiled=True)
-    pieces, target = kernel(make_fields, arrays((N_PLANE, 8 * TRACES, LANES), (2, 32, LANES)), 8)(
+    pieces, target = kernel(
+        make_fields,
+        [jax.ShapeDtypeStruct((N_PLANE, 16, LANES), jnp.int32)] + arrays((2, 32, LANES)),
+        8,
+    )(
         pieces, below, extra, above
     )
     pieces = lax.all_to_all(pieces, PLANE, 0, 0, tiled=True)
     (pieces,) = kernel(
         powers,
-        arrays((N_PLANE, 24, LANES)),
+        arrays((N_PLANE * ROWS, LANES)),
         8,
         scratch_shapes=[
             pltpu.VMEM((2, DEPTH, SUB, LANES), F32),
             pltpu.VMEM((ITERS + 1, 2, DEPTH, SUB, LANES), F32),
         ],
     )(pieces)
-    pieces = lax.all_to_all(pieces, PLANE, 0, 0, tiled=True)
-    (sums,) = kernel(spread_sums, arrays((N_GROUP, SUB, LANES)), 4)(pieces)
-    sums = lax.all_to_all(sums, GROUP, 0, 0, tiled=True)
+    pieces = exchange(pieces, PLANE, ROWS)
+    (sums,) = kernel(spread_sums, arrays((N_GROUP, LANES)), 4)(pieces)
+    sums = exchange(sums, GROUP, 1)
     shift, residual, again = kernel(
         combine,
         arrays((1, 1, 16, 512), (1, 1, 16, 512)) + [jax.ShapeDtypeStruct((1,), jnp.int32)],

time: 91.1 us -> 85.4 us (0.937)
  blocking collectives: 58.1 us -> 52.6 us
    all_to_all x2 -> x1, blocking collectives: 41.1 us -> 21.2 us  [per_device(): pieces = lax.all_to_all(pieces, PLANE, 0, 0, tiled=True)]
    all_to_all x1 -> x2, blocking collectives: 17 us -> 31.4 us  [exchange(): lax.all_to_all(rows.reshape(-1, count, 1, LANES), axes, 0, 0, tiled=True)]
where the time goes in v3:
time: 85.4 us; the launch traced here: 84.8 us
  blocking collectives  52.6 us (62%)
  starting transfers between devices  19.2 us (22%)
  Pallas kernels  7.93 us (9%)
  waiting for transfers between devices  2.65 us (3%)
  between operations  0.9 us (1%)
    all_to_all x2, blocking collectives, exchange(): lax.all_to_all(rows.reshape(-1, count, 1, LANES), axes, 0, 0, tiled=True)  31.4 us
    all_to_all x1, blocking collectives, per_device(): pieces = lax.all_to_all(pieces, PLANE, 0, 0, tiled=True)  21.2 us
    all_to_all x1, starting transfers between devices, per_device(): pieces = lax.all_to_all(pieces, GROUP, 0, 0, tiled=True)  11.8 us
    ppermute x1, starting transfers between devices, per_device(): above = lax.ppermute(extra, GROUP, [(i + 1, i) for i in range(N_GROUP - 1)])  4.07 us
    ppermute x1, starting transfers between devices, per_device(): below = lax.ppermute(extra, GROUP, [(i, i + 1) for i in range(N_GROUP - 1)])  3.28 us
    pallas_call x1, Pallas kernels, per_device(): kernel(powers, arrays((N_PLANE * ROWS, LANES)), 8, scratch_shapes=[pltpu....  2.47 us
    pallas_call x1, Pallas kernels, per_device(): kernel(make_fields, [jax.ShapeDtypeStruct((N_PLANE, 16, LANES), jnp.int32...  2.18 us
    ppermute x1, waiting for transfers between devices, per_device(): below = lax.ppermute(extra, GROUP, [(i, i + 1) for i in range(N_GROUP - 1)])  1.79 us
  transfers between devices with their start and end apart: 3, of which 3 were waited for; matrix products, arithmetic and copies ran while one was open for 0% of the time, Pallas kernels for 0%

profile of v3, /device:TPU:1, one launch (start us, length us, event | category | flops | bytes accessed | tf_op | source)
XLA Modules:
  0.0 84.8 jit_solution(6344437303928291406)
XLA Ops:
  0.6 1.6 %pack_inputs.1 = (f32[16,32,128]{2,1,0:T(8,128)}, f32[24,512]{1,0:T(8,128)}) custom-call(f32[4,1,16,128]{3,2,1,0:T(8,128)} %base_ref.1, f32[4,1,16,128]{3,2,1,0:T(8,128)} %mon_ref.1, s32[1,2,2,4]{3,2,1,0:T(2,128)} %bitcast.109, f32[1,1,16,512]{3,2,1,0:T(8,128)} %quality_ref.1), custom_call_target="tpu_custom_call" | custom-call | tf_op jit(solution)/shard_map/pack_inputs/pallas_call | solution.py:552
  2.2 11.8 %all-to-all-start.2 = ((f32[16,32,128]{2,1,0:T(8,128)}), f32[16,32,128]{2,1,0:T(8,128)S(1)}, u32[]{:S(2)}, u32[]{:S(2)}) async-start(f32[16,32,128]{2,1,0:T(8,128)} %get-tuple-element.44), calls=%async_computation.2 | async-start | bytes 524288 | tf_op jit(solution)/shard_map/all_to_all | solution.py:560
  14.0 3.3 %collective-permute-start.34 = (f32[24,512]{1,0:T(8,128)}, f32[24,512]{1,0:T(8,128)S(1)}, u32[]{:S(2)}, u32[]{:S(2)}) collective-permute-start(f32[24,512]{1,0:T(8,128)} %get-tuple-element.45.own_ref), channel_id=1, source_target_pairs={{0,32},{32,64},{64,96},{96,128},{128,160},{160,192},{192,224},{224... | collective-permute-start | bytes 147464 | tf_op jit(solution)/shard_map/ppermute | solution.py:558
  17.3 4.1 %collective-permute-start.35 = (f32[24,512]{1,0:T(8,128)}, f32[24,512]{1,0:T(8,128)S(1)}, u32[]{:S(2)}, u32[]{:S(2)}) collective-permute-start(f32[24,512]{1,0:T(8,128)} %get-tuple-element.45.own_ref), channel_id=1, source_target_pairs={{32,0},{64,32},{96,64},{128,96},{160,128},{192,160},{224,192},{256... | collective-permute-start | bytes 147464 | tf_op jit(solution)/shard_map/ppermute | solution.py:559
  21.4 1.8 %collective-permute-done.34.below_ref = f32[24,512]{1,0:T(8,128)S(1)} collective-permute-done((f32[24,512]{1,0:T(8,128)}, f32[24,512]{1,0:T(8,128)S(1)}, u32[]{:S(2)}, u32[]{:S(2)}) %collective-permute-start.34) | collective-permute-done | bytes 49184 | tf_op jit(solution)/shard_map/ppermute | solution.py:558
  23.2 0.6 collective-permute-done.35.above_ref
  23.8 0.2 all-to-all-done.2.recv_ref
  24.1 0.0 copy-start
  24.1 0.8 copy-done
  24.9 2.2 %make_fields.1 = (s32[32,16,128]{2,1,0:T(8,128)S(1)}, f32[2,32,128]{2,1,0:T(8,128)S(1)}) custom-call(f32[16,32,128]{2,1,0:T(8,128)S(1)} %all-to-all-done.2.recv_ref, f32[24,512]{1,0:T(8,128)S(1)} %collective-permute-done.34.below_ref, f32[24,512]{1,0:T(8,128)S(1)} %copy-done, f32[24,512]{1,0:T(8,128)S(1)} %collective-permute-done.35.above_ref), custom_call_target="tpu_custom_call" | custom-call | tf_op jit(solution)/shard_map/make_fields/pallas_call | solution.py:561
  27.0 0.0 copy-start.3
  27.1 0.0 copy-start.4
  27.1 0.0 copy-start.7
  27.1 21.2 %all_to_all.45.recv_ref = s32[32,16,128]{2,1,0:T(8,128)S(1)} all-to-all(s32[32,16,128]{2,1,0:T(8,128)S(1)} %get-tuple-element.46), channel_id=1, replica_groups=mesh['zh'=2,'core'=2,'zl'=4,'y'=8,'x'=4] {'y','x'}, dimensions={0} | all-to-all | bytes 524288 | tf_op jit(solution)/shard_map/all_to_all | solution.py:568
  48.2 2.5 %powers.1 = f32[544,128]{1,0:T(8,128)S(1)} custom-call(s32[32,16,128]{2,1,0:T(8,128)S(1)} %all_to_all.45.recv_ref), custom_call_target="tpu_custom_call" | custom-call | tf_op jit(solution)/shard_map/powers/pallas_call | solution.py:569
  50.7 15.1 %all_to_all.46 = f32[32,17,1,128]{3,2,1,0:T(1,128)S(1)} all-to-all(f32[32,17,1,128]{3,2,1,0:T(1,128)S(1)} %bitcast.93), channel_id=1, replica_groups=mesh['zh'=2,'core'=2,'zl'=4,'y'=8,'x'=4] {'y','x'}, dimensions={0} | all-to-all | bytes 557056 | tf_op jit(solution)/shard_map/all_to_all | solution.py:541
  65.9 16.3 %all_to_all.47 = f32[16,1,1,128]{3,2,1,0:T(1,128)S(1)} all-to-all(f32[16,1,1,128]{3,2,1,0:T(1,128)S(1)} %bitcast.95), channel_id=1, replica_groups=mesh['zh'=2,'core'=2,'zl'=4,'y'=8,'x'=4] {'zh','core','zl'}, dimensions={0} | all-to-all | bytes 16384 | tf_op jit(solution)/shard_map/all_to_all | solution.py:541
  82.1 1.7 %combine.1 = (f32[1,1,16,512]{3,2,1,0:T(8,128)}, f32[1,1,16,512]{3,2,1,0:T(8,128)}, s32[1]{0:T(128)}) custom-call(f32[544,128]{1,0:T(8,128)S(1)} %bitcast.92, f32[16,128]{1,0:T(8,128)S(1)} %bitcast.94, f32[2,32,128]{2,1,0:T(8,128)S(1)} %get-tuple-element.47.target_ref), custom_call_target="tpu_custom_call" | custom-call | tf_op jit(solution)/shard_map/combine/pallas_call | solution.py:581
  83.8 0.0 copy-done.3
  83.8 0.0 copy-done.4
  83.9 0.0 copy-done.7
  83.9 0.8 while.11
  (1 shorter events, 0.0 us)
Async XLA Ops:
  2.2 21.9 %all-to-all-start.2 = ((f32[16,32,128]{2,1,0:T(8,128)}), f32[16,32,128]{2,1,0:T(8,128)S(1)}, u32[]{:S(2)}, u32[]{:S(2)}) async-start(f32[16,32,128]{2,1,0:T(8,128)} %get-tuple-element.44), calls=%async_computation.2 | async-start | bytes 524288 | tf_op jit(solution)/shard_map/all_to_all | solution.py:560
  14.0 9.1 %collective-permute-start.34 = (f32[24,512]{1,0:T(8,128)}, f32[24,512]{1,0:T(8,128)S(1)}, u32[]{:S(2)}, u32[]{:S(2)}) collective-permute-start(f32[24,512]{1,0:T(8,128)} %get-tuple-element.45.own_ref), channel_id=1, source_target_pairs={{0,32},{32,64},{64,96},{96,128},{128,160},{160,192},{192,224},{224... | collective-permute-start | bytes 147464 | tf_op jit(solution)/shard_map/ppermute | solution.py:558
  17.3 6.5 %collective-permute-start.35 = (f32[24,512]{1,0:T(8,128)}, f32[24,512]{1,0:T(8,128)S(1)}, u32[]{:S(2)}, u32[]{:S(2)}) collective-permute-start(f32[24,512]{1,0:T(8,128)} %get-tuple-element.45.own_ref), channel_id=1, source_target_pairs={{32,0},{64,32},{96,64},{128,96},{160,128},{192,160},{224,192},{256... | collective-permute-start | bytes 147464 | tf_op jit(solution)/shard_map/ppermute | solution.py:559
  24.1 0.8 copy-start
  27.0 56.8 %copy-start.3 = (f32[4,1,16,128]{3,2,1,0:T(8,128)S(1)}, f32[4,1,16,128]{3,2,1,0:T(8,128)}, u32[]{:S(2)}) copy-start(f32[4,1,16,128]{3,2,1,0:T(8,128)} %base_ref.1) | copy-start | bytes 98308
  27.1 56.8 %copy-start.4 = (f32[4,1,16,128]{3,2,1,0:T(8,128)S(1)}, f32[4,1,16,128]{3,2,1,0:T(8,128)}, u32[]{:S(2)}) copy-start(f32[4,1,16,128]{3,2,1,0:T(8,128)} %mon_ref.1) | copy-start | bytes 98308
  27.1 56.8 %copy-start.7 = (s32[4,1,2,2]{0,3,2,1:T(2,128)S(1)}, s32[4,1,2,2]{0,3,2,1:T(2,128)}, u32[]{:S(2)}) copy-start(s32[4,1,2,2]{0,3,2,1:T(2,128)} %param.8) | copy-start | bytes 196

commit v4 on v3

--- a/solution.py
+++ b/solution.py
@@ -27,6 +27,7 @@
 FILT, IL = ("zh", "core"), ("zl", "y")
 LAGS = 128
 TRUST = 3e-4
+HBM = pl.BlockSpec(memory_space=pltpu.HBM)
 VMEM = pl.BlockSpec(memory_space=pltpu.VMEM)
 SMEM = pl.BlockSpec(memory_space=pltpu.SMEM)
 F32 = jnp.float32
@@ -44,15 +45,31 @@
     return pltpu.roll(value, amount, axis) if amount else value
 
 
-def pack_inputs(base_ref, mon_ref, bands_ref, quality_ref, out_ref, extra_ref):
+def pack_inputs(
+    base_hbm, mon_hbm, quality_hbm, bands_hbm, out_ref, extra_ref, base_ref, mon_ref, bands_ref, sems
+):
+    copies = [
+        pltpu.make_async_copy(source, target, sems.at[k])
+        for k, (source, target) in enumerate(
+            (
+                (bands_hbm, bands_ref),
+                (base_hbm, base_ref),
+                (mon_hbm, mon_ref),
+                (quality_hbm.at[0, 0], extra_ref.at[0:16]),
+            )
+        )
+    ]
+    for copy in copies:
+        copy.start()
     zl = lax.axis_index("zl")
     quarter = lax.axis_index("zh") * 2 + lax.axis_index("core")
+    for copy in copies:
+        copy.wait()
     for group in range(N_GROUP):
         offset = ((zl - group % 4 + 1) & 3) - 1
         source = jnp.clip(group + offset, 0, N_GROUP - 1) >> 2
         out_ref[group, 0:16, :] = base_ref[source, 0]
         out_ref[group, 16:32, :] = mon_ref[source, 0]
-    extra_ref[0:16, :] = quality_ref[0, 0]
     rows = lax.broadcasted_iota(jnp.int32, (SUB, 512), 0)
     bands = jnp.zeros((SUB, 512), F32)
     for block in range(2):
@@ -158,6 +175,11 @@
             out_ref[piece, at * 8 : at * 8 + 8, :] = packed
 
 
+def swap_halves(low, high, lane):
+    turned = roll(jnp.where(lane < 64, high, low), 64, 1)
+    return jnp.where(lane < 64, low, turned), jnp.where(lane < 64, turned, high)
+
+
 def beside(values, lane, row):
     low, high = values
     next_low, next_high = roll(low, 7, 1), roll(high, 7, 1)
@@ -174,6 +196,15 @@
 
 
 CHUNK = 2
+
+
+def chunks(begin, end):
+    out = []
+    while begin < end:
+        stop = min(end, begin + CHUNK, (begin // 8 + 1) * 8)
+        out.append((begin, stop))
+        begin = stop
+    return out
 
 
 def powers(recv_ref, out_ref, diag_ref, basis_ref):
@@ -201,35 +232,21 @@
             for at in range(2):
                 even = recv_ref[y * 4 + 2 * v, at * 8 : at * 8 + 8, :]
                 odd = recv_ref[y * 4 + 2 * v + 1, at * 8 : at * 8 + 8, :]
-                joined.append(jnp.where(lane < 64, even, roll(odd, 64, 1)))
-                joined.append(jnp.where(lane < 64, roll(even, 64, 1), odd))
+                joined += swap_halves(even, odd, lane)
             place(8 + y, joined[0].astype(F32) * (1.0 / FIXED), joined[1].astype(F32) * (1.0 / FIXED))
             place(y, *decode(joined[2]))
             place(16 + y, *decode(joined[3]))
-    lane3 = lax.broadcasted_iota(jnp.int32, (CHUNK, SUB, LANES), 2)
-    row3 = lax.broadcasted_iota(jnp.int32, (CHUNK, SUB, LANES), 1)
     own = (tau >= 8) & (tau < 24)
     squares, crosses = [], []
     for level in range(ITERS):
-        square = jnp.zeros((CHUNK, SUB, LANES), F32)
-        cross = jnp.zeros((CHUNK, SUB, LANES), F32)
-        begin = level + 1 + ((level + 1) % CHUNK and -1)
-        for inline in range(begin, DEPTH - begin, CHUNK):
-            region = inline // 8
-            here = slice(inline, inline + CHUNK)
+        square = jnp.zeros((SUB, LANES), F32)
+        cross = jnp.zeros((SUB, LANES), F32)
+        for begin, end in chunks(level + 1, DEPTH - 1 - level):
+            region, here = begin // 8, slice(begin, end)
             centre = [basis_ref[level, v, here] for v in range(2)]
-            sides = beside(centre, lane3, row3)
+            sides = beside(centre, lane[None], row[None])
             for v in range(2):
-                if inline == 0:
-                    inlines = jnp.concatenate([jnp.zeros((1, SUB, LANES), F32), basis_ref[level, v, 0 : CHUNK - 1]], axis=0)
-                else:
-                    inlines = basis_ref[level, v, inline - 1 : inline - 1 + CHUNK]
-                if inline + CHUNK == DEPTH:
-                    inlines = inlines + jnp.concatenate(
-                        [basis_ref[level, v, inline + 1 : DEPTH], jnp.zeros((1, SUB, LANES), F32)], axis=0
-                    )
-                else:
-                    inlines = inlines + basis_ref[level, v, inline + 1 : inline + 1 + CHUNK]
+                inlines = basis_ref[level, v, begin - 1 : end - 1] + basis_ref[level, v, begin + 1 : end + 1]
                 times = roll(centre[v], 1, 2) + roll(centre[v], LANES - 1, 2)
                 image = (
                     diag_ref[v, here] * centre[v]
@@ -239,10 +256,10 @@
                 image = 0.5 * image if level == 0 else image - basis_ref[level - 1, v, here]
                 basis_ref[level + 1, v, here] = image
                 if region == 1:
-                    square += centre[v] * centre[v]
-                    cross += centre[v] * image
-        squares.append(jnp.where(own, jnp.sum(square, axis=0), 0.0))
-        crosses.append(jnp.where(own, jnp.sum(cross, axis=0), 0.0))
+                    square += jnp.sum(centre[v] * centre[v], axis=0)
+                    cross += jnp.sum(centre[v] * image, axis=0)
+        squares.append(jnp.where(own, square, 0.0))
+        crosses.append(jnp.where(own, cross, 0.0))
     tiles = []
     for values in (squares, crosses):
         for amount in (4, 2, 1):
@@ -270,16 +287,12 @@
                         roll(basis_ref[k + 1, v, 8 + y], 8, 1),
                     )
                 )
-            turned = [roll(pair, 64, 1) for pair in pairs]
-            for half in range(2):
-                low, high = (pairs, turned) if half == 0 else (turned, pairs)
-                piece = y * 4 + 2 * v + half
-                for part in range(2):
-                    at = piece * ROWS + part * 8
-                    out_ref[at : at + 8, :] = jnp.where(
-                        lane < 64, low[2 * part], high[2 * part + 1]
-                    )
-                out_ref[piece * ROWS + 16 : piece * ROWS + 17, :] = tile[0:1]
+            for part in range(2):
+                for half, tile_half in enumerate(swap_halves(*pairs[2 * part : 2 * part + 2], lane)):
+                    at = (y * 4 + 2 * v + half) * ROWS + part * 8
+                    out_ref[at : at + 8, :] = tile_half
+    for piece in range(N_PLANE):
+        out_ref[piece * ROWS + 16 : piece * ROWS + 17, :] = tile[0:1]
 
 
 def spread_sums(recv_ref, out_ref):
@@ -420,19 +433,27 @@
             for k in (1, 5)
         )
         for part in range(4):
-            packed = [None, None]
-            for step in range(8):
-                piece = part * 8 + step
-                at = piece * ROWS
-                value = low * basis_ref[at : at + 8, :] + high * basis_ref[at + 8 : at + 16, :]
-                value = value + roll(value, 64, 1)
-                value = value + roll(value, 112, 1)
-                for h in range(2):
-                    turned = roll(value, (16 * step - 32 * h) % LANES, 1)
-                    packed[h] = turned if step == 0 else jnp.where(lane < 16 * step, packed[h], turned)
+            def piece(step):
+                at = (part * 8 + step) * ROWS
+                return low * basis_ref[at : at + 8, :] + high * basis_ref[at + 8 : at + 16, :]
+
+            def quad(step):
+                halves = []
+                for near in (step, step + 1):
+                    a, b = piece(near), piece(near + 4)
+                    halves.append(jnp.where(lane < 64, a, b) + roll(jnp.where(lane < 64, b, a), 64, 1))
+                a, b = halves
+                return jnp.where(first, a + roll(a, 112, 1), b + roll(b, 16, 1))
+
+            even, odd = quad(0), quad(2)
+            lower = (lane & 32) == 0
+            blocks = (
+                jnp.where(lower, even, roll(odd, 32, 1)),
+                jnp.where(lower, roll(even, 96, 1), odd),
+            )
             for h in range(2):
                 out_ref[0, 0, h * 8 : h * 8 + 8, part * LANES : (part + 1) * LANES] = (
-                    packed[h] + terms[0] * target_ref[h, part * 8 : part * 8 + 8, :]
+                    blocks[h] + terms[0] * target_ref[h, part * 8 : part * 8 + 8, :]
                 )
 
 
@@ -549,12 +570,18 @@
 
 
 def per_device(baseline, monitor, band_ids, quality):
-    pieces, extra = pl.pallas_call(
+    pieces, extra = kernel(
         pack_inputs,
-        out_shape=arrays((N_GROUP, 32, LANES), (DEPTH, 512)),
-        in_specs=[VMEM, VMEM, SMEM, VMEM],
-        name="pack_inputs",
-    )(baseline, monitor, band_ids.transpose(1, 2, 3, 0), quality)
+        arrays((N_GROUP, 32, LANES), (24, 512)),
+        4,
+        in_specs=[HBM] * 4,
+        scratch_shapes=[
+            pltpu.VMEM((4, 1, 16, LANES), F32),
+            pltpu.VMEM((4, 1, 16, LANES), F32),
+            pltpu.SMEM((1, 2, KB, 4), jnp.int32),
+            pltpu.SemaphoreType.DMA((4,)),
+        ],
+    )(baseline, monitor, quality, band_ids.transpose(1, 2, 3, 0))
     below = lax.ppermute(extra, GROUP, [(i, i + 1) for i in range(N_GROUP - 1)])
     above = lax.ppermute(extra, GROUP, [(i + 1, i) for i in range(N_GROUP - 1)])
     pieces = lax.all_to_all(pieces, GROUP, 0, 0, tiled=True)

time: 85.4 us -> 84 us (0.984)
  no operation moved by 1% of the time
where the time goes in v4:
time: 84 us; the launch traced here: 83.5 us
  blocking collectives  52.2 us (62%)
  starting transfers between devices  19.2 us (23%)
  Pallas kernels  7.72 us (9%)
  waiting for transfers between devices  2.71 us (3%)
  between operations  0.9 us (1%)
    all_to_all x2, blocking collectives, exchange(): lax.all_to_all(rows.reshape(-1, count, 1, LANES), axes, 0, 0, tiled=True)  31 us
    all_to_all x1, blocking collectives, per_device(): pieces = lax.all_to_all(pieces, PLANE, 0, 0, tiled=True)  21.2 us
    all_to_all x1, starting transfers between devices, per_device(): pieces = lax.all_to_all(pieces, GROUP, 0, 0, tiled=True)  11.8 us
    ppermute x1, starting transfers between devices, per_device(): above = lax.ppermute(extra, GROUP, [(i + 1, i) for i in range(N_GROUP - 1)])  4.07 us
    ppermute x1, starting transfers between devices, per_device(): below = lax.ppermute(extra, GROUP, [(i, i + 1) for i in range(N_GROUP - 1)])  3.28 us
    pallas_call x1, Pallas kernels, per_device(): kernel(powers, arrays((N_PLANE * ROWS, LANES)), 8, scratch_shapes=[pltpu....  2.39 us
    pallas_call x1, Pallas kernels, per_device(): kernel(make_fields, [jax.ShapeDtypeStruct((N_PLANE, 16, LANES), jnp.int32...  2.18 us
    ppermute x1, waiting for transfers between devices, per_device(): below = lax.ppermute(extra, GROUP, [(i, i + 1) for i in range(N_GROUP - 1)])  1.78 us
  transfers between devices with their start and end apart: 3, of which 3 were waited for; matrix products, arithmetic and copies ran while one was open for 0% of the time, Pallas kernels for 0%

profile of v4, /device:TPU:1, one launch (start us, length us, event | category | flops | bytes accessed | tf_op | source)
XLA Modules:
  0.0 83.5 jit_solution(2459652395598049505)
XLA Ops:
  0.6 1.5 %pack_inputs.1 = (f32[16,32,128]{2,1,0:T(8,128)}, f32[24,512]{1,0:T(8,128)S(1)}) custom-call(f32[4,1,16,128]{3,2,1,0:T(8,128)} %base_hbm.1, f32[4,1,16,128]{3,2,1,0:T(8,128)} %mon_hbm.1, f32[1,1,16,512]{3,2,1,0:T(8,128)} %quality_hbm.1, s32[1,2,2,4]{3,2,1,0:T(2,128)} %bitcast.109), custom_call_target="tpu_custom_call" | custom-call | tf_op jit(solution)/shard_map/pack_inputs/pallas_call | solution.py:573
  2.2 11.8 %all-to-all-start.2 = ((f32[16,32,128]{2,1,0:T(8,128)}), f32[16,32,128]{2,1,0:T(8,128)S(1)}, u32[]{:S(2)}, u32[]{:S(2)}) async-start(f32[16,32,128]{2,1,0:T(8,128)} %get-tuple-element.44), calls=%async_computation.2 | async-start | bytes 524288 | tf_op jit(solution)/shard_map/all_to_all | solution.py:587
  14.0 3.3 %collective-permute-start.34 = (f32[24,512]{1,0:T(8,128)S(1)}, f32[24,512]{1,0:T(8,128)S(1)}, u32[]{:S(2)}, u32[]{:S(2)}) collective-permute-start(f32[24,512]{1,0:T(8,128)S(1)} %get-tuple-element.45.own_ref), channel_id=1, source_target_pairs={{0,32},{32,64},{64,96},{96,128},{128,160},{160,192},{192,224},{224... | collective-permute-start | bytes 147464 | tf_op jit(solution)/shard_map/ppermute | solution.py:585
  17.3 4.1 %collective-permute-start.35 = (f32[24,512]{1,0:T(8,128)S(1)}, f32[24,512]{1,0:T(8,128)S(1)}, u32[]{:S(2)}, u32[]{:S(2)}) collective-permute-start(f32[24,512]{1,0:T(8,128)S(1)} %get-tuple-element.45.own_ref), channel_id=1, source_target_pairs={{32,0},{64,32},{96,64},{128,96},{160,128},{192,160},{224,192},{256... | collective-permute-start | bytes 147464 | tf_op jit(solution)/shard_map/ppermute | solution.py:586
  21.4 1.8 %collective-permute-done.34.below_ref = f32[24,512]{1,0:T(8,128)S(1)} collective-permute-done((f32[24,512]{1,0:T(8,128)S(1)}, f32[24,512]{1,0:T(8,128)S(1)}, u32[]{:S(2)}, u32[]{:S(2)}) %collective-permute-start.34) | collective-permute-done | bytes 49184 | tf_op jit(solution)/shard_map/ppermute | solution.py:585
  23.2 0.6 collective-permute-done.35.above_ref
  23.8 0.3 all-to-all-done.2.recv_ref
  24.1 2.2 %make_fields.1 = (s32[32,16,128]{2,1,0:T(8,128)S(1)}, f32[2,32,128]{2,1,0:T(8,128)S(1)}) custom-call(f32[16,32,128]{2,1,0:T(8,128)S(1)} %all-to-all-done.2.recv_ref, f32[24,512]{1,0:T(8,128)S(1)} %collective-permute-done.34.below_ref, f32[24,512]{1,0:T(8,128)S(1)} %get-tuple-element.45.own_ref, f32[24,512]{1,0:T(8,128)S(1)} %collective-permute-done.35.above_ref), custom_call_target="tpu_custom_call" | custom-call | tf_op jit(solution)/shard_map/make_fields/pallas_call | solution.py:588
  26.3 0.0 copy-start.2
  26.3 0.0 copy-start.3
  26.3 0.0 copy-start.6
  26.3 21.2 %all_to_all.45.recv_ref = s32[32,16,128]{2,1,0:T(8,128)S(1)} all-to-all(s32[32,16,128]{2,1,0:T(8,128)S(1)} %get-tuple-element.46), channel_id=1, replica_groups=mesh['zh'=2,'core'=2,'zl'=4,'y'=8,'x'=4] {'y','x'}, dimensions={0} | all-to-all | bytes 524288 | tf_op jit(solution)/shard_map/all_to_all | solution.py:595
  47.5 2.4 %powers.1 = f32[544,128]{1,0:T(8,128)S(1)} custom-call(s32[32,16,128]{2,1,0:T(8,128)S(1)} %all_to_all.45.recv_ref), custom_call_target="tpu_custom_call" | custom-call | tf_op jit(solution)/shard_map/powers/pallas_call | solution.py:596
  49.9 15.0 %all_to_all.46 = f32[32,17,1,128]{3,2,1,0:T(1,128)S(1)} all-to-all(f32[32,17,1,128]{3,2,1,0:T(1,128)S(1)} %bitcast.93), channel_id=1, replica_groups=mesh['zh'=2,'core'=2,'zl'=4,'y'=8,'x'=4] {'y','x'}, dimensions={0} | all-to-all | bytes 557056 | tf_op jit(solution)/shard_map/all_to_all | solution.py:562
  65.0 16.0 %all_to_all.47 = f32[16,1,1,128]{3,2,1,0:T(1,128)S(1)} all-to-all(f32[16,1,1,128]{3,2,1,0:T(1,128)S(1)} %bitcast.95), channel_id=1, replica_groups=mesh['zh'=2,'core'=2,'zl'=4,'y'=8,'x'=4] {'zh','core','zl'}, dimensions={0} | all-to-all | bytes 16384 | tf_op jit(solution)/shard_map/all_to_all | solution.py:562
  81.0 1.6 %combine.1 = (f32[1,1,16,512]{3,2,1,0:T(8,128)}, f32[1,1,16,512]{3,2,1,0:T(8,128)}, s32[1]{0:T(128)}) custom-call(f32[544,128]{1,0:T(8,128)S(1)} %bitcast.92, f32[16,128]{1,0:T(8,128)S(1)} %bitcast.94, f32[2,32,128]{2,1,0:T(8,128)S(1)} %get-tuple-element.47.target_ref), custom_call_target="tpu_custom_call" | custom-call | tf_op jit(solution)/shard_map/combine/pallas_call | solution.py:608
  82.5 0.0 copy-done.2
  82.6 0.0 copy-done.3
  82.6 0.0 copy-done.6
  82.6 0.8 while.11
  (1 shorter events, 0.0 us)
Async XLA Ops:
  2.2 21.9 %all-to-all-start.2 = ((f32[16,32,128]{2,1,0:T(8,128)}), f32[16,32,128]{2,1,0:T(8,128)S(1)}, u32[]{:S(2)}, u32[]{:S(2)}) async-start(f32[16,32,128]{2,1,0:T(8,128)} %get-tuple-element.44), calls=%async_computation.2 | async-start | bytes 524288 | tf_op jit(solution)/shard_map/all_to_all | solution.py:587
  14.0 9.1 %collective-permute-start.34 = (f32[24,512]{1,0:T(8,128)S(1)}, f32[24,512]{1,0:T(8,128)S(1)}, u32[]{:S(2)}, u32[]{:S(2)}) collective-permute-start(f32[24,512]{1,0:T(8,128)S(1)} %get-tuple-element.45.own_ref), channel_id=1, source_target_pairs={{0,32},{32,64},{64,96},{96,128},{128,160},{160,192},{192,224},{224... | collective-permute-start | bytes 147464 | tf_op jit(solution)/shard_map/ppermute | solution.py:585
  17.3 6.4 %collective-permute-start.35 = (f32[24,512]{1,0:T(8,128)S(1)}, f32[24,512]{1,0:T(8,128)S(1)}, u32[]{:S(2)}, u32[]{:S(2)}) collective-permute-start(f32[24,512]{1,0:T(8,128)S(1)} %get-tuple-element.45.own_ref), channel_id=1, source_target_pairs={{32,0},{64,32},{96,64},{128,96},{160,128},{192,160},{224,192},{256... | collective-permute-start | bytes 147464 | tf_op jit(solution)/shard_map/ppermute | solution.py:586
  26.3 56.3 %copy-start.2 = (f32[4,1,16,128]{3,2,1,0:T(8,128)S(1)}, f32[4,1,16,128]{3,2,1,0:T(8,128)}, u32[]{:S(2)}) copy-start(f32[4,1,16,128]{3,2,1,0:T(8,128)} %base_hbm.1) | copy-start | bytes 98308
  26.3 56.3 %copy-start.3 = (f32[4,1,16,128]{3,2,1,0:T(8,128)S(1)}, f32[4,1,16,128]{3,2,1,0:T(8,128)}, u32[]{:S(2)}) copy-start(f32[4,1,16,128]{3,2,1,0:T(8,128)} %mon_hbm.1) | copy-start | bytes 98308
  26.3 56.2 %copy-start.6 = (s32[4,1,2,2]{0,3,2,1:T(2,128)S(1)}, s32[4,1,2,2]{0,3,2,1:T(2,128)}, u32[]{:S(2)}) copy-start(s32[4,1,2,2]{0,3,2,1:T(2,128)} %param.8) | copy-start | bytes 196

commit v5 on v4

--- a/solution.py
+++ b/solution.py
@@ -22,11 +22,10 @@
 N_GROUP = 16
 N_PLANE = 32
 ROWS = 17
-FIXED = 2.0**29
 DEPTH = 24
 FILT, IL = ("zh", "core"), ("zl", "y")
 LAGS = 128
-TRUST = 3e-4
+TRUST = 1e-4
 HBM = pl.BlockSpec(memory_space=pltpu.HBM)
 VMEM = pl.BlockSpec(memory_space=pltpu.VMEM)
 SMEM = pl.BlockSpec(memory_space=pltpu.SMEM)
@@ -116,28 +115,14 @@
     return [jnp.where(lane < 8, sides[i], sides[i + 1]) for i in range(5)]
 
 
-def code(weight, target):
-    high = (jnp.sqrt(weight * 0.5) * 65535.0 + 0.5).astype(jnp.int32)
-    low = (jnp.sqrt(jnp.sqrt(jnp.abs(target) * 0.5)) * 32767.0 + 0.5).astype(jnp.int32)
-    low = jnp.where(target < 0.0, -low, low)
-    return (high << 16) | (low & 65535)
-
-
-def decode(coded):
-    high = lax.shift_right_logical(coded, 16).astype(F32) * (2.0**0.5 / 65535.0)
-    low = ((coded << 16) >> 16).astype(F32) * (2.0**0.25 / 32767.0)
-    return high * high, low * jnp.abs(low) * (low * low)
-
-
 def make_fields(recv_ref, below_ref, own_ref, above_ref, out_ref, target_ref):
     zl = lax.axis_index("zl")
     lane32 = lax.broadcasted_iota(jnp.int32, (32, LANES), 1)
     lane = lane_ids()
     zero = jnp.zeros((SUB, LANES), F32)
-    empty = jnp.zeros((SUB, LANES), jnp.int32)
-    exact, coded = [None] * 4, []
     for trace, extra_ref in enumerate((below_ref, own_ref, above_ref)):
         slot0 = (zl + trace - 1) & 3
+        fields = [None] * 4
         for block in range(2):
             rows = slice(block * 8, block * 8 + 8)
             mon_rows = slice(16 + block * 8, 24 + block * 8)
@@ -158,11 +143,8 @@
             weight, moment = weight * quality, moment * quality
             if trace == 1:
                 target_ref[block] = moment
-                exact[block] = spread((weight * FIXED).astype(jnp.int32), lane, empty)
-                exact[2 + block] = spread((moment * FIXED).astype(jnp.int32), lane, empty)
-            else:
-                coded.append(spread(code(weight, moment), lane, empty))
-    for at, fields in enumerate((exact, coded)):
+            fields[block] = spread(weight, lane, zero)
+            fields[2 + block] = spread(moment, lane, zero)
         for piece in range(N_PLANE):
             part, offset = piece // 8, 16 * (piece % 8)
             packed = None
@@ -172,7 +154,7 @@
                 if piece % 8 == 7:
                     value = jnp.where(lane < 32 * g + 16, value, roll(vregs[part + 1], shift, 1))
                 packed = value if packed is None else jnp.where(lane < 32 * g, packed, value)
-            out_ref[piece, at * 8 : at * 8 + 8, :] = packed
+            out_ref[piece, trace * 8 : trace * 8 + 8, :] = packed
 
 
 def swap_halves(low, high, lane):
@@ -221,21 +203,14 @@
     ]
     space = [share * (2.0 * smooth_space / CENTRE) for share in shares]
     along = [share * (2.0 * smooth_time / CENTRE) for share in shares]
-    def place(inline, weight, target):
-        centre = weight + (4.0 * smooth_space + 2.0 * smooth_time - CENTRE)
-        diag_ref[v, inline] = centre * (shares[inline // 8] * (2.0 / CENTRE))
-        basis_ref[0, v, inline] = target
-
-    for y in range(8):
+    for inline in range(DEPTH):
+        rows = slice(inline // 8 * 8, inline // 8 * 8 + 8)
         for v in range(2):
-            joined = []
-            for at in range(2):
-                even = recv_ref[y * 4 + 2 * v, at * 8 : at * 8 + 8, :]
-                odd = recv_ref[y * 4 + 2 * v + 1, at * 8 : at * 8 + 8, :]
-                joined += swap_halves(even, odd, lane)
-            place(8 + y, joined[0].astype(F32) * (1.0 / FIXED), joined[1].astype(F32) * (1.0 / FIXED))
-            place(y, *decode(joined[2]))
-            place(16 + y, *decode(joined[3]))
+            piece = inline % 8 * 4 + 2 * v
+            weight, target = swap_halves(recv_ref[piece, rows, :], recv_ref[piece + 1, rows, :], lane)
+            centre = weight + (4.0 * smooth_space + 2.0 * smooth_time - CENTRE)
+            diag_ref[v, inline] = centre * (shares[inline // 8] * (2.0 / CENTRE))
+            basis_ref[0, v, inline] = target
     own = (tau >= 8) & (tau < 24)
     squares, crosses = [], []
     for level in range(ITERS):
@@ -396,7 +371,7 @@
     parts = [split(pair[0]) for pair in gram]
     series = (apply_inverse(gram[0][0]), zero)
     steps = []
-    for _ in range(2):
+    for _ in range(1):
         body, top = remainder(series)
         high, low = zero, zero
         for k in range(ITERS + 1):
@@ -587,7 +562,7 @@
     pieces = lax.all_to_all(pieces, GROUP, 0, 0, tiled=True)
     pieces, target = kernel(
         make_fields,
-        [jax.ShapeDtypeStruct((N_PLANE, 16, LANES), jnp.int32)] + arrays((2, 32, LANES)),
+        arrays((N_PLANE, DEPTH, LANES), (2, 32, LANES)),
         8,
     )(
         pieces, below, extra, above

time: 84 us -> 86.7 us (1.032)
  blocking collectives: 52.2 us -> 54.9 us
    all_to_all x1, blocking collectives: 21.2 us -> 23.3 us  [per_device(): pieces = lax.all_to_all(pieces, PLANE, 0, 0, tiled=True)]
where the time goes in v5:
time: 86.7 us; the launch traced here: 86.3 us
  blocking collectives  54.9 us (63%)
  starting transfers between devices  19.2 us (22%)
  Pallas kernels  7.82 us (9%)
  waiting for transfers between devices  2.71 us (3%)
  between operations  0.88 us (1%)
    all_to_all x2, blocking collectives, exchange(): lax.all_to_all(rows.reshape(-1, count, 1, LANES), axes, 0, 0, tiled=True)  31.5 us
    all_to_all x1, blocking collectives, per_device(): pieces = lax.all_to_all(pieces, PLANE, 0, 0, tiled=True)  23.3 us
    all_to_all x1, starting transfers between devices, per_device(): pieces = lax.all_to_all(pieces, GROUP, 0, 0, tiled=True)  11.8 us
    ppermute x1, starting transfers between devices, per_device(): above = lax.ppermute(extra, GROUP, [(i + 1, i) for i in range(N_GROUP - 1)])  4.07 us
    ppermute x1, starting transfers between devices, per_device(): below = lax.ppermute(extra, GROUP, [(i, i + 1) for i in range(N_GROUP - 1)])  3.28 us
    pallas_call x1, Pallas kernels, per_device(): kernel(make_fields, arrays((N_PLANE, DEPTH, LANES), (2, 32, LANES)), 8)  2.41 us
    pallas_call x1, Pallas kernels, per_device(): kernel(powers, arrays((N_PLANE * ROWS, LANES)), 8, scratch_shapes=[pltpu....  2.35 us
    ppermute x1, waiting for transfers between devices, per_device(): below = lax.ppermute(extra, GROUP, [(i, i + 1) for i in range(N_GROUP - 1)])  1.78 us
  transfers between devices with their start and end apart: 3, of which 3 were waited for; matrix products, arithmetic and copies ran while one was open for 0% of the time, Pallas kernels for 0%

profile of v5, /device:TPU:1, one launch (start us, length us, event | category | flops | bytes accessed | tf_op | source)
XLA Modules:
  0.0 86.3 jit_solution(9829350728488568410)
XLA Ops:
  0.6 1.5 %pack_inputs.1 = (f32[16,32,128]{2,1,0:T(8,128)}, f32[24,512]{1,0:T(8,128)S(1)}) custom-call(f32[4,1,16,128]{3,2,1,0:T(8,128)} %base_hbm.1, f32[4,1,16,128]{3,2,1,0:T(8,128)} %mon_hbm.1, f32[1,1,16,512]{3,2,1,0:T(8,128)} %quality_hbm.1, s32[1,2,2,4]{3,2,1,0:T(2,128)} %bitcast.109), custom_call_target="tpu_custom_call" | custom-call | tf_op jit(solution)/shard_map/pack_inputs/pallas_call | solution.py:548
  2.2 11.8 %all-to-all-start.2 = ((f32[16,32,128]{2,1,0:T(8,128)}), f32[16,32,128]{2,1,0:T(8,128)S(1)}, u32[]{:S(2)}, u32[]{:S(2)}) async-start(f32[16,32,128]{2,1,0:T(8,128)} %get-tuple-element.44), calls=%async_computation.2 | async-start | bytes 524288 | tf_op jit(solution)/shard_map/all_to_all | solution.py:562
  14.0 3.3 %collective-permute-start.34 = (f32[24,512]{1,0:T(8,128)S(1)}, f32[24,512]{1,0:T(8,128)S(1)}, u32[]{:S(2)}, u32[]{:S(2)}) collective-permute-start(f32[24,512]{1,0:T(8,128)S(1)} %get-tuple-element.45.own_ref), channel_id=1, source_target_pairs={{0,32},{32,64},{64,96},{96,128},{128,160},{160,192},{192,224},{224... | collective-permute-start | bytes 147464 | tf_op jit(solution)/shard_map/ppermute | solution.py:560
  17.3 4.1 %collective-permute-start.35 = (f32[24,512]{1,0:T(8,128)S(1)}, f32[24,512]{1,0:T(8,128)S(1)}, u32[]{:S(2)}, u32[]{:S(2)}) collective-permute-start(f32[24,512]{1,0:T(8,128)S(1)} %get-tuple-element.45.own_ref), channel_id=1, source_target_pairs={{32,0},{64,32},{96,64},{128,96},{160,128},{192,160},{224,192},{256... | collective-permute-start | bytes 147464 | tf_op jit(solution)/shard_map/ppermute | solution.py:561
  21.4 1.8 %collective-permute-done.34.below_ref = f32[24,512]{1,0:T(8,128)S(1)} collective-permute-done((f32[24,512]{1,0:T(8,128)S(1)}, f32[24,512]{1,0:T(8,128)S(1)}, u32[]{:S(2)}, u32[]{:S(2)}) %collective-permute-start.34) | collective-permute-done | bytes 49184 | tf_op jit(solution)/shard_map/ppermute | solution.py:560
  23.2 0.6 collective-permute-done.35.above_ref
  23.8 0.3 all-to-all-done.2.recv_ref
  24.1 2.4 %make_fields.1 = (f32[32,24,128]{2,1,0:T(8,128)S(1)}, f32[2,32,128]{2,1,0:T(8,128)S(1)}) custom-call(f32[16,32,128]{2,1,0:T(8,128)S(1)} %all-to-all-done.2.recv_ref, f32[24,512]{1,0:T(8,128)S(1)} %collective-permute-done.34.below_ref, f32[24,512]{1,0:T(8,128)S(1)} %get-tuple-element.45.own_ref, f32[24,512]{1,0:T(8,128)S(1)} %collective-permute-done.35.above_ref), custom_call_target="tpu_custom_call" | custom-call | tf_op jit(solution)/shard_map/make_fields/pallas_call | solution.py:563
  26.5 23.3 %all_to_all.45.recv_ref = f32[32,24,128]{2,1,0:T(8,128)S(1)} all-to-all(f32[32,24,128]{2,1,0:T(8,128)S(1)} %get-tuple-element.46), channel_id=1, replica_groups=mesh['zh'=2,'core'=2,'zl'=4,'y'=8,'x'=4] {'y','x'}, dimensions={0} | all-to-all | bytes 786432 | tf_op jit(solution)/shard_map/all_to_all | solution.py:570
  49.9 0.0 copy-start.2
  49.9 0.0 copy-start.3
  49.9 0.0 copy-start.6
  49.9 2.3 %powers.1 = f32[544,128]{1,0:T(8,128)S(1)} custom-call(f32[32,24,128]{2,1,0:T(8,128)S(1)} %all_to_all.45.recv_ref), custom_call_target="tpu_custom_call" | custom-call | tf_op jit(solution)/shard_map/powers/pallas_call | solution.py:571
  52.2 15.4 %all_to_all.46 = f32[32,17,1,128]{3,2,1,0:T(1,128)S(1)} all-to-all(f32[32,17,1,128]{3,2,1,0:T(1,128)S(1)} %bitcast.93), channel_id=1, replica_groups=mesh['zh'=2,'core'=2,'zl'=4,'y'=8,'x'=4] {'y','x'}, dimensions={0} | all-to-all | bytes 557056 | tf_op jit(solution)/shard_map/all_to_all | solution.py:537
  67.7 16.1 %all_to_all.47 = f32[16,1,1,128]{3,2,1,0:T(1,128)S(1)} all-to-all(f32[16,1,1,128]{3,2,1,0:T(1,128)S(1)} %bitcast.95), channel_id=1, replica_groups=mesh['zh'=2,'core'=2,'zl'=4,'y'=8,'x'=4] {'zh','core','zl'}, dimensions={0} | all-to-all | bytes 16384 | tf_op jit(solution)/shard_map/all_to_all | solution.py:537
  83.8 1.5 %combine.1 = (f32[1,1,16,512]{3,2,1,0:T(8,128)}, f32[1,1,16,512]{3,2,1,0:T(8,128)}, s32[1]{0:T(128)}) custom-call(f32[544,128]{1,0:T(8,128)S(1)} %bitcast.92, f32[16,128]{1,0:T(8,128)S(1)} %bitcast.94, f32[2,32,128]{2,1,0:T(8,128)S(1)} %get-tuple-element.47.target_ref), custom_call_target="tpu_custom_call" | custom-call | tf_op jit(solution)/shard_map/combine/pallas_call | solution.py:583
  85.3 0.0 copy-done.2
  85.3 0.0 copy-done.3
  85.3 0.0 copy-done.6
  85.3 0.8 while.11
  (1 shorter events, 0.0 us)
Async XLA Ops:
  2.2 21.9 %all-to-all-start.2 = ((f32[16,32,128]{2,1,0:T(8,128)}), f32[16,32,128]{2,1,0:T(8,128)S(1)}, u32[]{:S(2)}, u32[]{:S(2)}) async-start(f32[16,32,128]{2,1,0:T(8,128)} %get-tuple-element.44), calls=%async_computation.2 | async-start | bytes 524288 | tf_op jit(solution)/shard_map/all_to_all | solution.py:562
  14.0 9.1 %collective-permute-start.34 = (f32[24,512]{1,0:T(8,128)S(1)}, f32[24,512]{1,0:T(8,128)S(1)}, u32[]{:S(2)}, u32[]{:S(2)}) collective-permute-start(f32[24,512]{1,0:T(8,128)S(1)} %get-tuple-element.45.own_ref), channel_id=1, source_target_pairs={{0,32},{32,64},{64,96},{96,128},{128,160},{160,192},{192,224},{224... | collective-permute-start | bytes 147464 | tf_op jit(solution)/shard_map/ppermute | solution.py:560
  17.3 6.4 %collective-permute-start.35 = (f32[24,512]{1,0:T(8,128)S(1)}, f32[24,512]{1,0:T(8,128)S(1)}, u32[]{:S(2)}, u32[]{:S(2)}) collective-permute-start(f32[24,512]{1,0:T(8,128)S(1)} %get-tuple-element.45.own_ref), channel_id=1, source_target_pairs={{32,0},{64,32},{96,64},{128,96},{160,128},{192,160},{224,192},{256... | collective-permute-start | bytes 147464 | tf_op jit(solution)/shard_map/ppermute | solution.py:561
  49.9 35.4 %copy-start.2 = (f32[4,1,16,128]{3,2,1,0:T(8,128)S(1)}, f32[4,1,16,128]{3,2,1,0:T(8,128)}, u32[]{:S(2)}) copy-start(f32[4,1,16,128]{3,2,1,0:T(8,128)} %base_hbm.1) | copy-start | bytes 98308
  49.9 35.4 %copy-start.3 = (f32[4,1,16,128]{3,2,1,0:T(8,128)S(1)}, f32[4,1,16,128]{3,2,1,0:T(8,128)}, u32[]{:S(2)}) copy-start(f32[4,1,16,128]{3,2,1,0:T(8,128)} %mon_hbm.1) | copy-start | bytes 98308
  49.9 35.4 %copy-start.6 = (s32[4,1,2,2]{0,3,2,1:T(2,128)S(1)}, s32[4,1,2,2]{0,3,2,1:T(2,128)}, u32[]{:S(2)}) copy-start(s32[4,1,2,2]{0,3,2,1:T(2,128)} %param.8) | copy-start | bytes 196

commit v6 on v5

--- a/solution.py
+++ b/solution.py
@@ -22,10 +22,11 @@
 N_GROUP = 16
 N_PLANE = 32
 ROWS = 17
+STEPS = 2.0**20 - 1.0
 DEPTH = 24
 FILT, IL = ("zh", "core"), ("zl", "y")
 LAGS = 128
-TRUST = 1e-4
+TRUST = 5e-5
 HBM = pl.BlockSpec(memory_space=pltpu.HBM)
 VMEM = pl.BlockSpec(memory_space=pltpu.VMEM)
 SMEM = pl.BlockSpec(memory_space=pltpu.SMEM)
@@ -115,14 +116,40 @@
     return [jnp.where(lane < 8, sides[i], sides[i + 1]) for i in range(5)]
 
 
+def words_of(fields):
+    weights = [(weight * STEPS + 0.5).astype(jnp.int32) for weight, _ in fields]
+    targets = []
+    for _, target in fields:
+        size = (jnp.sqrt(jnp.abs(target) * 0.5) * STEPS + 0.5).astype(jnp.int32)
+        targets.append(jnp.where(target < 0.0, -size, size))
+    words = []
+    for low, own, high in (weights, targets):
+        words += [(low << 11) | ((high >> 10) & 2047), (own << 11) | (high & 1023)]
+    return words
+
+
+def fields_of(words):
+    a, b, c, d = words
+    weights = [lax.shift_right_logical(part, 11) for part in (a, b)]
+    weights.append(((a & 2047) << 10) | (b & 1023))
+    targets = [c >> 11, d >> 11]
+    targets.append(((((c & 2047) << 10) | (d & 1023)) << 11) >> 11)
+    out = []
+    for weight, target in zip(weights, targets):
+        root = target.astype(F32) * (2.0**0.5 / STEPS)
+        out.append((weight.astype(F32) * (1.0 / STEPS), root * jnp.abs(root)))
+    return out
+
+
 def make_fields(recv_ref, below_ref, own_ref, above_ref, out_ref, target_ref):
     zl = lax.axis_index("zl")
     lane32 = lax.broadcasted_iota(jnp.int32, (32, LANES), 1)
     lane = lane_ids()
     zero = jnp.zeros((SUB, LANES), F32)
+    empty = jnp.zeros((SUB, LANES), jnp.int32)
+    fields = [[], []]
     for trace, extra_ref in enumerate((below_ref, own_ref, above_ref)):
         slot0 = (zl + trace - 1) & 3
-        fields = [None] * 4
         for block in range(2):
             rows = slice(block * 8, block * 8 + 8)
             mon_rows = slice(16 + block * 8, 24 + block * 8)
@@ -143,18 +170,20 @@
             weight, moment = weight * quality, moment * quality
             if trace == 1:
                 target_ref[block] = moment
-            fields[block] = spread(weight, lane, zero)
-            fields[2 + block] = spread(moment, lane, zero)
+            fields[block].append((weight, moment))
+    words = [[spread(word, lane, empty) for word in words_of(part)] for part in fields]
+    for at in range(2):
+        groups = [words[h][2 * at + k] for k in range(2) for h in range(2)]
         for piece in range(N_PLANE):
             part, offset = piece // 8, 16 * (piece % 8)
             packed = None
-            for g, vregs in enumerate(fields):
+            for g, vregs in enumerate(groups):
                 shift = (32 * g - offset) % LANES
                 value = roll(vregs[part], shift, 1)
                 if piece % 8 == 7:
                     value = jnp.where(lane < 32 * g + 16, value, roll(vregs[part + 1], shift, 1))
                 packed = value if packed is None else jnp.where(lane < 32 * g, packed, value)
-            out_ref[piece, trace * 8 : trace * 8 + 8, :] = packed
+            out_ref[piece, at * 8 : at * 8 + 8, :] = packed
 
 
 def swap_halves(low, high, lane):
@@ -203,14 +232,16 @@
     ]
     space = [share * (2.0 * smooth_space / CENTRE) for share in shares]
     along = [share * (2.0 * smooth_time / CENTRE) for share in shares]
-    for inline in range(DEPTH):
-        rows = slice(inline // 8 * 8, inline // 8 * 8 + 8)
+    for y in range(8):
         for v in range(2):
-            piece = inline % 8 * 4 + 2 * v
-            weight, target = swap_halves(recv_ref[piece, rows, :], recv_ref[piece + 1, rows, :], lane)
-            centre = weight + (4.0 * smooth_space + 2.0 * smooth_time - CENTRE)
-            diag_ref[v, inline] = centre * (shares[inline // 8] * (2.0 / CENTRE))
-            basis_ref[0, v, inline] = target
+            piece = y * 4 + 2 * v
+            words = []
+            for rows in (slice(0, 8), slice(8, 16)):
+                words += swap_halves(recv_ref[piece, rows, :], recv_ref[piece + 1, rows, :], lane)
+            for trace, (weight, target) in enumerate(fields_of(words)):
+                centre = weight + (4.0 * smooth_space + 2.0 * smooth_time - CENTRE)
+                diag_ref[v, trace * 8 + y] = centre * (shares[trace] * (2.0 / CENTRE))
+                basis_ref[0, v, trace * 8 + y] = target
     own = (tau >= 8) & (tau < 24)
     squares, crosses = [], []
     for level in range(ITERS):
@@ -562,7 +593,7 @@
     pieces = lax.all_to_all(pieces, GROUP, 0, 0, tiled=True)
     pieces, target = kernel(
         make_fields,
-        arrays((N_PLANE, DEPTH, LANES), (2, 32, LANES)),
+        [jax.ShapeDtypeStruct((N_PLANE, 16, LANES), jnp.int32)] + arrays((2, 32, LANES)),
         8,
     )(
         pieces, below, extra, above

time: 86.7 us -> 83.5 us (0.963)
  blocking collectives: 54.9 us -> 52.2 us
    all_to_all x1, blocking collectives: 23.3 us -> 21.2 us  [per_device(): pieces = lax.all_to_all(pieces, PLANE, 0, 0, tiled=True)]
where the time goes in v6:
time: 83.5 us; the launch traced here: 83.1 us
  blocking collectives  52.2 us (63%)
  starting transfers between devices  19.2 us (23%)
  Pallas kernels  7.23 us (9%)
  waiting for transfers between devices  2.71 us (3%)
  between operations  0.9 us (1%)
    all_to_all x2, blocking collectives, exchange(): lax.all_to_all(rows.reshape(-1, count, 1, LANES), axes, 0, 0, tiled=True)  31 us
    all_to_all x1, blocking collectives, per_device(): pieces = lax.all_to_all(pieces, PLANE, 0, 0, tiled=True)  21.2 us
    all_to_all x1, starting transfers between devices, per_device(): pieces = lax.all_to_all(pieces, GROUP, 0, 0, tiled=True)  11.8 us
    ppermute x1, starting transfers between devices, per_device(): above = lax.ppermute(extra, GROUP, [(i + 1, i) for i in range(N_GROUP - 1)])  4.07 us
    ppermute x1, starting transfers between devices, per_device(): below = lax.ppermute(extra, GROUP, [(i, i + 1) for i in range(N_GROUP - 1)])  3.28 us
    pallas_call x1, Pallas kernels, per_device(): kernel(powers, arrays((N_PLANE * ROWS, LANES)), 8, scratch_shapes=[pltpu....  2.38 us
    ppermute x1, waiting for transfers between devices, per_device(): below = lax.ppermute(extra, GROUP, [(i, i + 1) for i in range(N_GROUP - 1)])  1.78 us
    pallas_call x1, Pallas kernels, per_device(): kernel(make_fields, [jax.ShapeDtypeStruct((N_PLANE, 16, LANES), jnp.int32...  1.77 us
  transfers between devices with their start and end apart: 3, of which 3 were waited for; matrix products, arithmetic and copies ran while one was open for 0% of the time, Pallas kernels for 0%

profile of v6, /device:TPU:1, one launch (start us, length us, event | category | flops | bytes accessed | tf_op | source)
XLA Modules:
  0.0 83.1 jit_solution(3331147758141565017)
XLA Ops:
  0.6 1.5 %pack_inputs.1 = (f32[16,32,128]{2,1,0:T(8,128)}, f32[24,512]{1,0:T(8,128)S(1)}) custom-call(f32[4,1,16,128]{3,2,1,0:T(8,128)} %base_hbm.1, f32[4,1,16,128]{3,2,1,0:T(8,128)} %mon_hbm.1, f32[1,1,16,512]{3,2,1,0:T(8,128)} %quality_hbm.1, s32[1,2,2,4]{3,2,1,0:T(2,128)} %bitcast.109), custom_call_target="tpu_custom_call" | custom-call | tf_op jit(solution)/shard_map/pack_inputs/pallas_call | solution.py:579
  2.2 11.8 %all-to-all-start.2 = ((f32[16,32,128]{2,1,0:T(8,128)}), f32[16,32,128]{2,1,0:T(8,128)S(1)}, u32[]{:S(2)}, u32[]{:S(2)}) async-start(f32[16,32,128]{2,1,0:T(8,128)} %get-tuple-element.44), calls=%async_computation.2 | async-start | bytes 524288 | tf_op jit(solution)/shard_map/all_to_all | solution.py:593
  14.0 3.3 %collective-permute-start.34 = (f32[24,512]{1,0:T(8,128)S(1)}, f32[24,512]{1,0:T(8,128)S(1)}, u32[]{:S(2)}, u32[]{:S(2)}) collective-permute-start(f32[24,512]{1,0:T(8,128)S(1)} %get-tuple-element.45.own_ref), channel_id=1, source_target_pairs={{0,32},{32,64},{64,96},{96,128},{128,160},{160,192},{192,224},{224... | collective-permute-start | bytes 147464 | tf_op jit(solution)/shard_map/ppermute | solution.py:591
  17.3 4.1 %collective-permute-start.35 = (f32[24,512]{1,0:T(8,128)S(1)}, f32[24,512]{1,0:T(8,128)S(1)}, u32[]{:S(2)}, u32[]{:S(2)}) collective-permute-start(f32[24,512]{1,0:T(8,128)S(1)} %get-tuple-element.45.own_ref), channel_id=1, source_target_pairs={{32,0},{64,32},{96,64},{128,96},{160,128},{192,160},{224,192},{256... | collective-permute-start | bytes 147464 | tf_op jit(solution)/shard_map/ppermute | solution.py:592
  21.4 1.8 %collective-permute-done.34.below_ref = f32[24,512]{1,0:T(8,128)S(1)} collective-permute-done((f32[24,512]{1,0:T(8,128)S(1)}, f32[24,512]{1,0:T(8,128)S(1)}, u32[]{:S(2)}, u32[]{:S(2)}) %collective-permute-start.34) | collective-permute-done | bytes 49184 | tf_op jit(solution)/shard_map/ppermute | solution.py:591
  23.2 0.6 collective-permute-done.35.above_ref
  23.8 0.3 all-to-all-done.2.recv_ref
  24.1 1.8 %make_fields.1 = (s32[32,16,128]{2,1,0:T(8,128)S(1)}, f32[2,32,128]{2,1,0:T(8,128)S(1)}) custom-call(f32[16,32,128]{2,1,0:T(8,128)S(1)} %all-to-all-done.2.recv_ref, f32[24,512]{1,0:T(8,128)S(1)} %collective-permute-done.34.below_ref, f32[24,512]{1,0:T(8,128)S(1)} %get-tuple-element.45.own_ref, f32[24,512]{1,0:T(8,128)S(1)} %collective-permute-done.35.above_ref), custom_call_target="tpu_custom_call" | custom-call | tf_op jit(solution)/shard_map/make_fields/pallas_call | solution.py:594
  25.9 0.0 copy-start.2
  25.9 0.0 copy-start.3
  25.9 0.0 copy-start.6
  25.9 21.2 %all_to_all.45.recv_ref = s32[32,16,128]{2,1,0:T(8,128)S(1)} all-to-all(s32[32,16,128]{2,1,0:T(8,128)S(1)} %get-tuple-element.46), channel_id=1, replica_groups=mesh['zh'=2,'core'=2,'zl'=4,'y'=8,'x'=4] {'y','x'}, dimensions={0} | all-to-all | bytes 524288 | tf_op jit(solution)/shard_map/all_to_all | solution.py:601
  47.1 2.4 %powers.1 = f32[544,128]{1,0:T(8,128)S(1)} custom-call(s32[32,16,128]{2,1,0:T(8,128)S(1)} %all_to_all.45.recv_ref), custom_call_target="tpu_custom_call" | custom-call | tf_op jit(solution)/shard_map/powers/pallas_call | solution.py:602
  49.5 15.0 %all_to_all.46 = f32[32,17,1,128]{3,2,1,0:T(1,128)S(1)} all-to-all(f32[32,17,1,128]{3,2,1,0:T(1,128)S(1)} %bitcast.93), channel_id=1, replica_groups=mesh['zh'=2,'core'=2,'zl'=4,'y'=8,'x'=4] {'y','x'}, dimensions={0} | all-to-all | bytes 557056 | tf_op jit(solution)/shard_map/all_to_all | solution.py:568
  64.5 16.0 %all_to_all.47 = f32[16,1,1,128]{3,2,1,0:T(1,128)S(1)} all-to-all(f32[16,1,1,128]{3,2,1,0:T(1,128)S(1)} %bitcast.95), channel_id=1, replica_groups=mesh['zh'=2,'core'=2,'zl'=4,'y'=8,'x'=4] {'zh','core','zl'}, dimensions={0} | all-to-all | bytes 16384 | tf_op jit(solution)/shard_map/all_to_all | solution.py:568
  80.5 1.5 %combine.1 = (f32[1,1,16,512]{3,2,1,0:T(8,128)}, f32[1,1,16,512]{3,2,1,0:T(8,128)}, s32[1]{0:T(128)}) custom-call(f32[544,128]{1,0:T(8,128)S(1)} %bitcast.92, f32[16,128]{1,0:T(8,128)S(1)} %bitcast.94, f32[2,32,128]{2,1,0:T(8,128)S(1)} %get-tuple-element.47.target_ref), custom_call_target="tpu_custom_call" | custom-call | tf_op jit(solution)/shard_map/combine/pallas_call | solution.py:614
  82.1 0.0 copy-done.2
  82.1 0.0 copy-done.3
  82.1 0.0 copy-done.6
  82.1 0.8 while.11
  (1 shorter events, 0.0 us)
Async XLA Ops:
  2.2 21.9 %all-to-all-start.2 = ((f32[16,32,128]{2,1,0:T(8,128)}), f32[16,32,128]{2,1,0:T(8,128)S(1)}, u32[]{:S(2)}, u32[]{:S(2)}) async-start(f32[16,32,128]{2,1,0:T(8,128)} %get-tuple-element.44), calls=%async_computation.2 | async-start | bytes 524288 | tf_op jit(solution)/shard_map/all_to_all | solution.py:593
  14.0 9.1 %collective-permute-start.34 = (f32[24,512]{1,0:T(8,128)S(1)}, f32[24,512]{1,0:T(8,128)S(1)}, u32[]{:S(2)}, u32[]{:S(2)}) collective-permute-start(f32[24,512]{1,0:T(8,128)S(1)} %get-tuple-element.45.own_ref), channel_id=1, source_target_pairs={{0,32},{32,64},{64,96},{96,128},{128,160},{160,192},{192,224},{224... | collective-permute-start | bytes 147464 | tf_op jit(solution)/shard_map/ppermute | solution.py:591
  17.3 6.4 %collective-permute-start.35 = (f32[24,512]{1,0:T(8,128)S(1)}, f32[24,512]{1,0:T(8,128)S(1)}, u32[]{:S(2)}, u32[]{:S(2)}) collective-permute-start(f32[24,512]{1,0:T(8,128)S(1)} %get-tuple-element.45.own_ref), channel_id=1, source_target_pairs={{32,0},{64,32},{96,64},{128,96},{160,128},{192,160},{224,192},{256... | collective-permute-start | bytes 147464 | tf_op jit(solution)/shard_map/ppermute | solution.py:592
  25.9 56.2 %copy-start.2 = (f32[4,1,16,128]{3,2,1,0:T(8,128)S(1)}, f32[4,1,16,128]{3,2,1,0:T(8,128)}, u32[]{:S(2)}) copy-start(f32[4,1,16,128]{3,2,1,0:T(8,128)} %base_hbm.1) | copy-start | bytes 98308
  25.9 56.2 %copy-start.3 = (f32[4,1,16,128]{3,2,1,0:T(8,128)S(1)}, f32[4,1,16,128]{3,2,1,0:T(8,128)}, u32[]{:S(2)}) copy-start(f32[4,1,16,128]{3,2,1,0:T(8,128)} %mon_hbm.1) | copy-start | bytes 98308
  25.9 56.2 %copy-start.6 = (s32[4,1,2,2]{0,3,2,1:T(2,128)S(1)}, s32[4,1,2,2]{0,3,2,1:T(2,128)}, u32[]{:S(2)}) copy-start(s32[4,1,2,2]{0,3,2,1:T(2,128)} %param.8) | copy-start | bytes 196

commit v7 on v6

--- a/solution.py
+++ b/solution.py
@@ -287,14 +287,10 @@
             pairs = []
             for k in range(1, 9, 2):
                 pairs.append(
-                    jnp.where(
-                        tau < 16,
-                        roll(basis_ref[k, v, 8 + y], 120, 1),
-                        roll(basis_ref[k + 1, v, 8 + y], 8, 1),
-                    )
+                    jnp.where(own, basis_ref[k, v, 8 + y], roll(basis_ref[k + 1, v, 8 + y], 16, 1))
                 )
             for part in range(2):
-                for half, tile_half in enumerate(swap_halves(*pairs[2 * part : 2 * part + 2], lane)):
+                for half, tile_half in enumerate(swap_halves(*pairs[2 * part : 2 * part + 2], (lane - 8) & 127)):
                     at = (y * 4 + 2 * v + half) * ROWS + part * 8
                     out_ref[at : at + 8, :] = tile_half
     for piece in range(N_PLANE):
@@ -427,6 +423,7 @@
     shift, residual, last, steps, series = solve(total, lane, row, roll)
     fine = jnp.max(jnp.abs(steps[0])) <= TRUST * jnp.max(jnp.abs(series))
     again_ref[0] = 1 - fine.astype(jnp.int32)
+    lane = (lane - 8) & 127
     first = (lane & 31) < 16
     for body, top, out_ref in ((shift, zero, shift_ref), (residual, last, residual_ref)):
         terms = [across(body, k) for k in range(ITERS)] + [top]
@@ -459,7 +456,7 @@
             )
             for h in range(2):
                 out_ref[0, 0, h * 8 : h * 8 + 8, part * LANES : (part + 1) * LANES] = (
-                    blocks[h] + terms[0] * target_ref[h, part * 8 : part * 8 + 8, :]
+                    roll(blocks[h], 120, 1) + terms[0] * target_ref[h, part * 8 : part * 8 + 8, :]
                 )
 
 

time: 83.5 us -> 83.2 us (level)
  no operation moved by 1% of the time
where the time goes in v7:
time: 83.2 us; the launch traced here: 82.7 us
  blocking collectives  52.2 us (63%)
  starting transfers between devices  19.2 us (23%)
  Pallas kernels  6.92 us (8%)
  waiting for transfers between devices  2.71 us (3%)
  between operations  0.9 us (1%)
    all_to_all x2, blocking collectives, exchange(): lax.all_to_all(rows.reshape(-1, count, 1, LANES), axes, 0, 0, tiled=True)  31 us
    all_to_all x1, blocking collectives, per_device(): pieces = lax.all_to_all(pieces, PLANE, 0, 0, tiled=True)  21.2 us
    all_to_all x1, starting transfers between devices, per_device(): pieces = lax.all_to_all(pieces, GROUP, 0, 0, tiled=True)  11.8 us
    ppermute x1, starting transfers between devices, per_device(): above = lax.ppermute(extra, GROUP, [(i + 1, i) for i in range(N_GROUP - 1)])  4.07 us
    ppermute x1, starting transfers between devices, per_device(): below = lax.ppermute(extra, GROUP, [(i, i + 1) for i in range(N_GROUP - 1)])  3.28 us
    pallas_call x1, Pallas kernels, per_device(): kernel(powers, arrays((N_PLANE * ROWS, LANES)), 8, scratch_shapes=[pltpu....  2.01 us
    ppermute x1, waiting for transfers between devices, per_device(): below = lax.ppermute(extra, GROUP, [(i, i + 1) for i in range(N_GROUP - 1)])  1.78 us
    pallas_call x1, Pallas kernels, per_device(): kernel(make_fields, [jax.ShapeDtypeStruct((N_PLANE, 16, LANES), jnp.int32...  1.77 us
  transfers between devices with their start and end apart: 3, of which 3 were waited for; matrix products, arithmetic and copies ran while one was open for 0% of the time, Pallas kernels for 0%

profile of v7, /device:TPU:1, one launch (start us, length us, event | category | flops | bytes accessed | tf_op | source)
XLA Modules:
  0.0 82.7 jit_solution(15358337784623417885)
XLA Ops:
  0.6 1.5 %pack_inputs.1 = (f32[16,32,128]{2,1,0:T(8,128)}, f32[24,512]{1,0:T(8,128)S(1)}) custom-call(f32[4,1,16,128]{3,2,1,0:T(8,128)} %base_hbm.1, f32[4,1,16,128]{3,2,1,0:T(8,128)} %mon_hbm.1, f32[1,1,16,512]{3,2,1,0:T(8,128)} %quality_hbm.1, s32[1,2,2,4]{3,2,1,0:T(2,128)} %bitcast.109), custom_call_target="tpu_custom_call" | custom-call | tf_op jit(solution)/shard_map/pack_inputs/pallas_call | solution.py:576
  2.2 11.8 %all-to-all-start.2 = ((f32[16,32,128]{2,1,0:T(8,128)}), f32[16,32,128]{2,1,0:T(8,128)S(1)}, u32[]{:S(2)}, u32[]{:S(2)}) async-start(f32[16,32,128]{2,1,0:T(8,128)} %get-tuple-element.44), calls=%async_computation.2 | async-start | bytes 524288 | tf_op jit(solution)/shard_map/all_to_all | solution.py:590
  14.0 3.3 %collective-permute-start.34 = (f32[24,512]{1,0:T(8,128)S(1)}, f32[24,512]{1,0:T(8,128)S(1)}, u32[]{:S(2)}, u32[]{:S(2)}) collective-permute-start(f32[24,512]{1,0:T(8,128)S(1)} %get-tuple-element.45.own_ref), channel_id=1, source_target_pairs={{0,32},{32,64},{64,96},{96,128},{128,160},{160,192},{192,224},{224... | collective-permute-start | bytes 147464 | tf_op jit(solution)/shard_map/ppermute | solution.py:588
  17.3 4.1 %collective-permute-start.35 = (f32[24,512]{1,0:T(8,128)S(1)}, f32[24,512]{1,0:T(8,128)S(1)}, u32[]{:S(2)}, u32[]{:S(2)}) collective-permute-start(f32[24,512]{1,0:T(8,128)S(1)} %get-tuple-element.45.own_ref), channel_id=1, source_target_pairs={{32,0},{64,32},{96,64},{128,96},{160,128},{192,160},{224,192},{256... | collective-permute-start | bytes 147464 | tf_op jit(solution)/shard_map/ppermute | solution.py:589
  21.4 1.8 %collective-permute-done.34.below_ref = f32[24,512]{1,0:T(8,128)S(1)} collective-permute-done((f32[24,512]{1,0:T(8,128)S(1)}, f32[24,512]{1,0:T(8,128)S(1)}, u32[]{:S(2)}, u32[]{:S(2)}) %collective-permute-start.34) | collective-permute-done | bytes 49184 | tf_op jit(solution)/shard_map/ppermute | solution.py:588
  23.2 0.6 collective-permute-done.35.above_ref
  23.8 0.3 all-to-all-done.2.recv_ref
  24.1 1.8 %make_fields.1 = (s32[32,16,128]{2,1,0:T(8,128)S(1)}, f32[2,32,128]{2,1,0:T(8,128)S(1)}) custom-call(f32[16,32,128]{2,1,0:T(8,128)S(1)} %all-to-all-done.2.recv_ref, f32[24,512]{1,0:T(8,128)S(1)} %collective-permute-done.34.below_ref, f32[24,512]{1,0:T(8,128)S(1)} %get-tuple-element.45.own_ref, f32[24,512]{1,0:T(8,128)S(1)} %collective-permute-done.35.above_ref), custom_call_target="tpu_custom_call" | custom-call | tf_op jit(solution)/shard_map/make_fields/pallas_call | solution.py:591
  25.9 0.0 copy-start.2
  25.9 0.0 copy-start.3
  25.9 0.0 copy-start.6
  25.9 21.2 %all_to_all.45.recv_ref = s32[32,16,128]{2,1,0:T(8,128)S(1)} all-to-all(s32[32,16,128]{2,1,0:T(8,128)S(1)} %get-tuple-element.46), channel_id=1, replica_groups=mesh['zh'=2,'core'=2,'zl'=4,'y'=8,'x'=4] {'y','x'}, dimensions={0} | all-to-all | bytes 524288 | tf_op jit(solution)/shard_map/all_to_all | solution.py:598
  47.1 2.0 %powers.1 = f32[544,128]{1,0:T(8,128)S(1)} custom-call(s32[32,16,128]{2,1,0:T(8,128)S(1)} %all_to_all.45.recv_ref), custom_call_target="tpu_custom_call" | custom-call | tf_op jit(solution)/shard_map/powers/pallas_call | solution.py:599
  49.1 15.0 %all_to_all.46 = f32[32,17,1,128]{3,2,1,0:T(1,128)S(1)} all-to-all(f32[32,17,1,128]{3,2,1,0:T(1,128)S(1)} %bitcast.93), channel_id=1, replica_groups=mesh['zh'=2,'core'=2,'zl'=4,'y'=8,'x'=4] {'y','x'}, dimensions={0} | all-to-all | bytes 557056 | tf_op jit(solution)/shard_map/all_to_all | solution.py:565
  64.2 16.0 %all_to_all.47 = f32[16,1,1,128]{3,2,1,0:T(1,128)S(1)} all-to-all(f32[16,1,1,128]{3,2,1,0:T(1,128)S(1)} %bitcast.95), channel_id=1, replica_groups=mesh['zh'=2,'core'=2,'zl'=4,'y'=8,'x'=4] {'zh','core','zl'}, dimensions={0} | all-to-all | bytes 16384 | tf_op jit(solution)/shard_map/all_to_all | solution.py:565
  80.2 1.6 %combine.1 = (f32[1,1,16,512]{3,2,1,0:T(8,128)}, f32[1,1,16,512]{3,2,1,0:T(8,128)}, s32[1]{0:T(128)}) custom-call(f32[544,128]{1,0:T(8,128)S(1)} %bitcast.92, f32[16,128]{1,0:T(8,128)S(1)} %bitcast.94, f32[2,32,128]{2,1,0:T(8,128)S(1)} %get-tuple-element.47.target_ref), custom_call_target="tpu_custom_call" | custom-call | tf_op jit(solution)/shard_map/combine/pallas_call | solution.py:611
  81.8 0.0 copy-done.2
  81.8 0.0 copy-done.3
  81.8 0.0 copy-done.6
  81.8 0.8 while.11
  (1 shorter events, 0.0 us)
Async XLA Ops:
  2.2 21.9 %all-to-all-start.2 = ((f32[16,32,128]{2,1,0:T(8,128)}), f32[16,32,128]{2,1,0:T(8,128)S(1)}, u32[]{:S(2)}, u32[]{:S(2)}) async-start(f32[16,32,128]{2,1,0:T(8,128)} %get-tuple-element.44), calls=%async_computation.2 | async-start | bytes 524288 | tf_op jit(solution)/shard_map/all_to_all | solution.py:590
  14.0 9.1 %collective-permute-start.34 = (f32[24,512]{1,0:T(8,128)S(1)}, f32[24,512]{1,0:T(8,128)S(1)}, u32[]{:S(2)}, u32[]{:S(2)}) collective-permute-start(f32[24,512]{1,0:T(8,128)S(1)} %get-tuple-element.45.own_ref), channel_id=1, source_target_pairs={{0,32},{32,64},{64,96},{96,128},{128,160},{160,192},{192,224},{224... | collective-permute-start | bytes 147464 | tf_op jit(solution)/shard_map/ppermute | solution.py:588
  17.3 6.4 %collective-permute-start.35 = (f32[24,512]{1,0:T(8,128)S(1)}, f32[24,512]{1,0:T(8,128)S(1)}, u32[]{:S(2)}, u32[]{:S(2)}) collective-permute-start(f32[24,512]{1,0:T(8,128)S(1)} %get-tuple-element.45.own_ref), channel_id=1, source_target_pairs={{32,0},{64,32},{96,64},{128,96},{160,128},{192,160},{224,192},{256... | collective-permute-start | bytes 147464 | tf_op jit(solution)/shard_map/ppermute | solution.py:589
  25.9 55.9 %copy-start.2 = (f32[4,1,16,128]{3,2,1,0:T(8,128)S(1)}, f32[4,1,16,128]{3,2,1,0:T(8,128)}, u32[]{:S(2)}) copy-start(f32[4,1,16,128]{3,2,1,0:T(8,128)} %base_hbm.1) | copy-start | bytes 98308
  25.9 55.9 %copy-start.3 = (f32[4,1,16,128]{3,2,1,0:T(8,128)S(1)}, f32[4,1,16,128]{3,2,1,0:T(8,128)}, u32[]{:S(2)}) copy-start(f32[4,1,16,128]{3,2,1,0:T(8,128)} %mon_hbm.1) | copy-start | bytes 98308
  25.9 55.9 %copy-start.6 = (s32[4,1,2,2]{0,3,2,1:T(2,128)S(1)}, s32[4,1,2,2]{0,3,2,1:T(2,128)}, u32[]{:S(2)}) copy-start(s32[4,1,2,2]{0,3,2,1:T(2,128)} %param.8) | copy-start | bytes 196

commit v8 on v7

--- a/solution.py
+++ b/solution.py
@@ -370,7 +370,7 @@
         gram.append(add_pairs(later, earlier))
     inverse = [gram[k][0] + 0.5 * (gram[k + 1][0] + gram[abs(k - 1)][0]) for k in range(ITERS)]
     for k in range(ITERS):
-        reciprocal = 1.0 / across(inverse[k], k)
+        reciprocal = pl.reciprocal(across(inverse[k], k), approx=False)
         pivot = inverse[k]
         for j in range(ITERS):
             if j != k:

time: 83.2 us -> 83.2 us (level)
  no operation moved by 1% of the time
where the time goes in v8:
time: 83.2 us; the launch traced here: 82.7 us
  blocking collectives  52.2 us (63%)
  starting transfers between devices  19.2 us (23%)
  Pallas kernels  6.92 us (8%)
  waiting for transfers between devices  2.71 us (3%)
  between operations  0.9 us (1%)
    all_to_all x2, blocking collectives, exchange(): lax.all_to_all(rows.reshape(-1, count, 1, LANES), axes, 0, 0, tiled=True)  31 us
    all_to_all x1, blocking collectives, per_device(): pieces = lax.all_to_all(pieces, PLANE, 0, 0, tiled=True)  21.2 us
    all_to_all x1, starting transfers between devices, per_device(): pieces = lax.all_to_all(pieces, GROUP, 0, 0, tiled=True)  11.8 us
    ppermute x1, starting transfers between devices, per_device(): above = lax.ppermute(extra, GROUP, [(i + 1, i) for i in range(N_GROUP - 1)])  4.07 us
    ppermute x1, starting transfers between devices, per_device(): below = lax.ppermute(extra, GROUP, [(i, i + 1) for i in range(N_GROUP - 1)])  3.28 us
    pallas_call x1, Pallas kernels, per_device(): kernel(powers, arrays((N_PLANE * ROWS, LANES)), 8, scratch_shapes=[pltpu....  2.01 us
    ppermute x1, waiting for transfers between devices, per_device(): below = lax.ppermute(extra, GROUP, [(i, i + 1) for i in range(N_GROUP - 1)])  1.78 us
    pallas_call x1, Pallas kernels, per_device(): kernel(make_fields, [jax.ShapeDtypeStruct((N_PLANE, 16, LANES), jnp.int32...  1.77 us
  transfers between devices with their start and end apart: 3, of which 3 were waited for; matrix products, arithmetic and copies ran while one was open for 0% of the time, Pallas kernels for 0%

profile of v8, /device:TPU:1, one launch (start us, length us, event | category | flops | bytes accessed | tf_op | source)
XLA Modules:
  0.0 82.7 jit_solution(15358337784623417885)
XLA Ops:
  0.6 1.5 %pack_inputs.1 = (f32[16,32,128]{2,1,0:T(8,128)}, f32[24,512]{1,0:T(8,128)S(1)}) custom-call(f32[4,1,16,128]{3,2,1,0:T(8,128)} %base_hbm.1, f32[4,1,16,128]{3,2,1,0:T(8,128)} %mon_hbm.1, f32[1,1,16,512]{3,2,1,0:T(8,128)} %quality_hbm.1, s32[1,2,2,4]{3,2,1,0:T(2,128)} %bitcast.109), custom_call_target="tpu_custom_call" | custom-call | tf_op jit(solution)/shard_map/pack_inputs/pallas_call | solution.py:576
  2.2 11.8 %all-to-all-start.2 = ((f32[16,32,128]{2,1,0:T(8,128)}), f32[16,32,128]{2,1,0:T(8,128)S(1)}, u32[]{:S(2)}, u32[]{:S(2)}) async-start(f32[16,32,128]{2,1,0:T(8,128)} %get-tuple-element.44), calls=%async_computation.2 | async-start | bytes 524288 | tf_op jit(solution)/shard_map/all_to_all | solution.py:590
  14.0 3.3 %collective-permute-start.34 = (f32[24,512]{1,0:T(8,128)S(1)}, f32[24,512]{1,0:T(8,128)S(1)}, u32[]{:S(2)}, u32[]{:S(2)}) collective-permute-start(f32[24,512]{1,0:T(8,128)S(1)} %get-tuple-element.45.own_ref), channel_id=1, source_target_pairs={{0,32},{32,64},{64,96},{96,128},{128,160},{160,192},{192,224},{224... | collective-permute-start | bytes 147464 | tf_op jit(solution)/shard_map/ppermute | solution.py:588
  17.3 4.1 %collective-permute-start.35 = (f32[24,512]{1,0:T(8,128)S(1)}, f32[24,512]{1,0:T(8,128)S(1)}, u32[]{:S(2)}, u32[]{:S(2)}) collective-permute-start(f32[24,512]{1,0:T(8,128)S(1)} %get-tuple-element.45.own_ref), channel_id=1, source_target_pairs={{32,0},{64,32},{96,64},{128,96},{160,128},{192,160},{224,192},{256... | collective-permute-start | bytes 147464 | tf_op jit(solution)/shard_map/ppermute | solution.py:589
  21.4 1.8 %collective-permute-done.34.below_ref = f32[24,512]{1,0:T(8,128)S(1)} collective-permute-done((f32[24,512]{1,0:T(8,128)S(1)}, f32[24,512]{1,0:T(8,128)S(1)}, u32[]{:S(2)}, u32[]{:S(2)}) %collective-permute-start.34) | collective-permute-done | bytes 49184 | tf_op jit(solution)/shard_map/ppermute | solution.py:588
  23.2 0.6 collective-permute-done.35.above_ref
  23.8 0.3 all-to-all-done.2.recv_ref
  24.1 1.8 %make_fields.1 = (s32[32,16,128]{2,1,0:T(8,128)S(1)}, f32[2,32,128]{2,1,0:T(8,128)S(1)}) custom-call(f32[16,32,128]{2,1,0:T(8,128)S(1)} %all-to-all-done.2.recv_ref, f32[24,512]{1,0:T(8,128)S(1)} %collective-permute-done.34.below_ref, f32[24,512]{1,0:T(8,128)S(1)} %get-tuple-element.45.own_ref, f32[24,512]{1,0:T(8,128)S(1)} %collective-permute-done.35.above_ref), custom_call_target="tpu_custom_call" | custom-call | tf_op jit(solution)/shard_map/make_fields/pallas_call | solution.py:591
  25.9 0.0 copy-start.2
  25.9 0.0 copy-start.3
  25.9 0.0 copy-start.6
  25.9 21.2 %all_to_all.45.recv_ref = s32[32,16,128]{2,1,0:T(8,128)S(1)} all-to-all(s32[32,16,128]{2,1,0:T(8,128)S(1)} %get-tuple-element.46), channel_id=1, replica_groups=mesh['zh'=2,'core'=2,'zl'=4,'y'=8,'x'=4] {'y','x'}, dimensions={0} | all-to-all | bytes 524288 | tf_op jit(solution)/shard_map/all_to_all | solution.py:598
  47.1 2.0 %powers.1 = f32[544,128]{1,0:T(8,128)S(1)} custom-call(s32[32,16,128]{2,1,0:T(8,128)S(1)} %all_to_all.45.recv_ref), custom_call_target="tpu_custom_call" | custom-call | tf_op jit(solution)/shard_map/powers/pallas_call | solution.py:599
  49.1 15.0 %all_to_all.46 = f32[32,17,1,128]{3,2,1,0:T(1,128)S(1)} all-to-all(f32[32,17,1,128]{3,2,1,0:T(1,128)S(1)} %bitcast.93), channel_id=1, replica_groups=mesh['zh'=2,'core'=2,'zl'=4,'y'=8,'x'=4] {'y','x'}, dimensions={0} | all-to-all | bytes 557056 | tf_op jit(solution)/shard_map/all_to_all | solution.py:565
  64.2 16.0 %all_to_all.47 = f32[16,1,1,128]{3,2,1,0:T(1,128)S(1)} all-to-all(f32[16,1,1,128]{3,2,1,0:T(1,128)S(1)} %bitcast.95), channel_id=1, replica_groups=mesh['zh'=2,'core'=2,'zl'=4,'y'=8,'x'=4] {'zh','core','zl'}, dimensions={0} | all-to-all | bytes 16384 | tf_op jit(solution)/shard_map/all_to_all | solution.py:565
  80.2 1.6 %combine.1 = (f32[1,1,16,512]{3,2,1,0:T(8,128)}, f32[1,1,16,512]{3,2,1,0:T(8,128)}, s32[1]{0:T(128)}) custom-call(f32[544,128]{1,0:T(8,128)S(1)} %bitcast.92, f32[16,128]{1,0:T(8,128)S(1)} %bitcast.94, f32[2,32,128]{2,1,0:T(8,128)S(1)} %get-tuple-element.47.target_ref), custom_call_target="tpu_custom_call" | custom-call | tf_op jit(solution)/shard_map/combine/pallas_call | solution.py:611
  81.8 0.0 copy-done.2
  81.8 0.0 copy-done.3
  81.8 0.0 copy-done.6
  81.8 0.8 while.11
  (1 shorter events, 0.0 us)
Async XLA Ops:
  2.2 21.9 %all-to-all-start.2 = ((f32[16,32,128]{2,1,0:T(8,128)}), f32[16,32,128]{2,1,0:T(8,128)S(1)}, u32[]{:S(2)}, u32[]{:S(2)}) async-start(f32[16,32,128]{2,1,0:T(8,128)} %get-tuple-element.44), calls=%async_computation.2 | async-start | bytes 524288 | tf_op jit(solution)/shard_map/all_to_all | solution.py:590
  14.0 9.1 %collective-permute-start.34 = (f32[24,512]{1,0:T(8,128)S(1)}, f32[24,512]{1,0:T(8,128)S(1)}, u32[]{:S(2)}, u32[]{:S(2)}) collective-permute-start(f32[24,512]{1,0:T(8,128)S(1)} %get-tuple-element.45.own_ref), channel_id=1, source_target_pairs={{0,32},{32,64},{64,96},{96,128},{128,160},{160,192},{192,224},{224... | collective-permute-start | bytes 147464 | tf_op jit(solution)/shard_map/ppermute | solution.py:588
  17.3 6.4 %collective-permute-start.35 = (f32[24,512]{1,0:T(8,128)S(1)}, f32[24,512]{1,0:T(8,128)S(1)}, u32[]{:S(2)}, u32[]{:S(2)}) collective-permute-start(f32[24,512]{1,0:T(8,128)S(1)} %get-tuple-element.45.own_ref), channel_id=1, source_target_pairs={{32,0},{64,32},{96,64},{128,96},{160,128},{192,160},{224,192},{256... | collective-permute-start | bytes 147464 | tf_op jit(solution)/shard_map/ppermute | solution.py:589
  25.9 55.9 %copy-start.2 = (f32[4,1,16,128]{3,2,1,0:T(8,128)S(1)}, f32[4,1,16,128]{3,2,1,0:T(8,128)}, u32[]{:S(2)}) copy-start(f32[4,1,16,128]{3,2,1,0:T(8,128)} %base_hbm.1) | copy-start | bytes 98308
  25.9 55.9 %copy-start.3 = (f32[4,1,16,128]{3,2,1,0:T(8,128)S(1)}, f32[4,1,16,128]{3,2,1,0:T(8,128)}, u32[]{:S(2)}) copy-start(f32[4,1,16,128]{3,2,1,0:T(8,128)} %mon_hbm.1) | copy-start | bytes 98308
  25.9 55.9 %copy-start.6 = (s32[4,1,2,2]{0,3,2,1:T(2,128)S(1)}, s32[4,1,2,2]{0,3,2,1:T(2,128)}, u32[]{:S(2)}) copy-start(s32[4,1,2,2]{0,3,2,1:T(2,128)} %param.8) | copy-start | bytes 196

commit v9 on v7

--- a/solution.py
+++ b/solution.py
@@ -206,7 +206,7 @@
     return up_low + down_low, up_high + down_high
 
 
-CHUNK = 2
+CHUNK = 4
 
 
 def chunks(begin, end):

time: 83.2 us -> 83.3 us (level)
  no operation moved by 1% of the time
where the time goes in v9:
time: 83.3 us; the launch traced here: 82.8 us
  blocking collectives  52.2 us (63%)
  starting transfers between devices  19.2 us (23%)
  Pallas kernels  6.97 us (8%)
  waiting for transfers between devices  2.71 us (3%)
  between operations  0.9 us (1%)
    all_to_all x2, blocking collectives, exchange(): lax.all_to_all(rows.reshape(-1, count, 1, LANES), axes, 0, 0, tiled=True)  31 us
    all_to_all x1, blocking collectives, per_device(): pieces = lax.all_to_all(pieces, PLANE, 0, 0, tiled=True)  21.2 us
    all_to_all x1, starting transfers between devices, per_device(): pieces = lax.all_to_all(pieces, GROUP, 0, 0, tiled=True)  11.8 us
    ppermute x1, starting transfers between devices, per_device(): above = lax.ppermute(extra, GROUP, [(i + 1, i) for i in range(N_GROUP - 1)])  4.07 us
    ppermute x1, starting transfers between devices, per_device(): below = lax.ppermute(extra, GROUP, [(i, i + 1) for i in range(N_GROUP - 1)])  3.28 us
    pallas_call x1, Pallas kernels, per_device(): kernel(powers, arrays((N_PLANE * ROWS, LANES)), 8, scratch_shapes=[pltpu....  2.06 us
    ppermute x1, waiting for transfers between devices, per_device(): below = lax.ppermute(extra, GROUP, [(i, i + 1) for i in range(N_GROUP - 1)])  1.78 us
    pallas_call x1, Pallas kernels, per_device(): kernel(make_fields, [jax.ShapeDtypeStruct((N_PLANE, 16, LANES), jnp.int32...  1.77 us
  transfers between devices with their start and end apart: 3, of which 3 were waited for; matrix products, arithmetic and copies ran while one was open for 0% of the time, Pallas kernels for 0%

profile of v9, /device:TPU:1, one launch (start us, length us, event | category | flops | bytes accessed | tf_op | source)
XLA Modules:
  0.0 82.8 jit_solution(2779508806327015242)
XLA Ops:
  0.6 1.5 %pack_inputs.1 = (f32[16,32,128]{2,1,0:T(8,128)}, f32[24,512]{1,0:T(8,128)S(1)}) custom-call(f32[4,1,16,128]{3,2,1,0:T(8,128)} %base_hbm.1, f32[4,1,16,128]{3,2,1,0:T(8,128)} %mon_hbm.1, f32[1,1,16,512]{3,2,1,0:T(8,128)} %quality_hbm.1, s32[1,2,2,4]{3,2,1,0:T(2,128)} %bitcast.109), custom_call_target="tpu_custom_call" | custom-call | tf_op jit(solution)/shard_map/pack_inputs/pallas_call | solution.py:576
  2.2 11.8 %all-to-all-start.2 = ((f32[16,32,128]{2,1,0:T(8,128)}), f32[16,32,128]{2,1,0:T(8,128)S(1)}, u32[]{:S(2)}, u32[]{:S(2)}) async-start(f32[16,32,128]{2,1,0:T(8,128)} %get-tuple-element.44), calls=%async_computation.2 | async-start | bytes 524288 | tf_op jit(solution)/shard_map/all_to_all | solution.py:590
  14.0 3.3 %collective-permute-start.34 = (f32[24,512]{1,0:T(8,128)S(1)}, f32[24,512]{1,0:T(8,128)S(1)}, u32[]{:S(2)}, u32[]{:S(2)}) collective-permute-start(f32[24,512]{1,0:T(8,128)S(1)} %get-tuple-element.45.own_ref), channel_id=1, source_target_pairs={{0,32},{32,64},{64,96},{96,128},{128,160},{160,192},{192,224},{224... | collective-permute-start | bytes 147464 | tf_op jit(solution)/shard_map/ppermute | solution.py:588
  17.3 4.1 %collective-permute-start.35 = (f32[24,512]{1,0:T(8,128)S(1)}, f32[24,512]{1,0:T(8,128)S(1)}, u32[]{:S(2)}, u32[]{:S(2)}) collective-permute-start(f32[24,512]{1,0:T(8,128)S(1)} %get-tuple-element.45.own_ref), channel_id=1, source_target_pairs={{32,0},{64,32},{96,64},{128,96},{160,128},{192,160},{224,192},{256... | collective-permute-start | bytes 147464 | tf_op jit(solution)/shard_map/ppermute | solution.py:589
  21.4 1.8 %collective-permute-done.34.below_ref = f32[24,512]{1,0:T(8,128)S(1)} collective-permute-done((f32[24,512]{1,0:T(8,128)S(1)}, f32[24,512]{1,0:T(8,128)S(1)}, u32[]{:S(2)}, u32[]{:S(2)}) %collective-permute-start.34) | collective-permute-done | bytes 49184 | tf_op jit(solution)/shard_map/ppermute | solution.py:588
  23.2 0.6 collective-permute-done.35.above_ref
  23.8 0.3 all-to-all-done.2.recv_ref
  24.1 1.8 %make_fields.1 = (s32[32,16,128]{2,1,0:T(8,128)S(1)}, f32[2,32,128]{2,1,0:T(8,128)S(1)}) custom-call(f32[16,32,128]{2,1,0:T(8,128)S(1)} %all-to-all-done.2.recv_ref, f32[24,512]{1,0:T(8,128)S(1)} %collective-permute-done.34.below_ref, f32[24,512]{1,0:T(8,128)S(1)} %get-tuple-element.45.own_ref, f32[24,512]{1,0:T(8,128)S(1)} %collective-permute-done.35.above_ref), custom_call_target="tpu_custom_call" | custom-call | tf_op jit(solution)/shard_map/make_fields/pallas_call | solution.py:591
  25.9 0.0 copy-start.2
  25.9 0.0 copy-start.3
  25.9 0.0 copy-start.6
  25.9 21.2 %all_to_all.45.recv_ref = s32[32,16,128]{2,1,0:T(8,128)S(1)} all-to-all(s32[32,16,128]{2,1,0:T(8,128)S(1)} %get-tuple-element.46), channel_id=1, replica_groups=mesh['zh'=2,'core'=2,'zl'=4,'y'=8,'x'=4] {'y','x'}, dimensions={0} | all-to-all | bytes 524288 | tf_op jit(solution)/shard_map/all_to_all | solution.py:598
  47.1 2.1 %powers.1 = f32[544,128]{1,0:T(8,128)S(1)} custom-call(s32[32,16,128]{2,1,0:T(8,128)S(1)} %all_to_all.45.recv_ref), custom_call_target="tpu_custom_call" | custom-call | tf_op jit(solution)/shard_map/powers/pallas_call | solution.py:599
  49.2 15.0 %all_to_all.46 = f32[32,17,1,128]{3,2,1,0:T(1,128)S(1)} all-to-all(f32[32,17,1,128]{3,2,1,0:T(1,128)S(1)} %bitcast.93), channel_id=1, replica_groups=mesh['zh'=2,'core'=2,'zl'=4,'y'=8,'x'=4] {'y','x'}, dimensions={0} | all-to-all | bytes 557056 | tf_op jit(solution)/shard_map/all_to_all | solution.py:565
  64.2 16.0 %all_to_all.47 = f32[16,1,1,128]{3,2,1,0:T(1,128)S(1)} all-to-all(f32[16,1,1,128]{3,2,1,0:T(1,128)S(1)} %bitcast.95), channel_id=1, replica_groups=mesh['zh'=2,'core'=2,'zl'=4,'y'=8,'x'=4] {'zh','core','zl'}, dimensions={0} | all-to-all | bytes 16384 | tf_op jit(solution)/shard_map/all_to_all | solution.py:565
  80.2 1.6 %combine.1 = (f32[1,1,16,512]{3,2,1,0:T(8,128)}, f32[1,1,16,512]{3,2,1,0:T(8,128)}, s32[1]{0:T(128)}) custom-call(f32[544,128]{1,0:T(8,128)S(1)} %bitcast.92, f32[16,128]{1,0:T(8,128)S(1)} %bitcast.94, f32[2,32,128]{2,1,0:T(8,128)S(1)} %get-tuple-element.47.target_ref), custom_call_target="tpu_custom_call" | custom-call | tf_op jit(solution)/shard_map/combine/pallas_call | solution.py:611
  81.8 0.0 copy-done.2
  81.8 0.0 copy-done.3
  81.8 0.0 copy-done.6
  81.8 0.8 while.11
  (1 shorter events, 0.0 us)
Async XLA Ops:
  2.2 21.9 %all-to-all-start.2 = ((f32[16,32,128]{2,1,0:T(8,128)}), f32[16,32,128]{2,1,0:T(8,128)S(1)}, u32[]{:S(2)}, u32[]{:S(2)}) async-start(f32[16,32,128]{2,1,0:T(8,128)} %get-tuple-element.44), calls=%async_computation.2 | async-start | bytes 524288 | tf_op jit(solution)/shard_map/all_to_all | solution.py:590
  14.0 9.1 %collective-permute-start.34 = (f32[24,512]{1,0:T(8,128)S(1)}, f32[24,512]{1,0:T(8,128)S(1)}, u32[]{:S(2)}, u32[]{:S(2)}) collective-permute-start(f32[24,512]{1,0:T(8,128)S(1)} %get-tuple-element.45.own_ref), channel_id=1, source_target_pairs={{0,32},{32,64},{64,96},{96,128},{128,160},{160,192},{192,224},{224... | collective-permute-start | bytes 147464 | tf_op jit(solution)/shard_map/ppermute | solution.py:588
  17.3 6.4 %collective-permute-start.35 = (f32[24,512]{1,0:T(8,128)S(1)}, f32[24,512]{1,0:T(8,128)S(1)}, u32[]{:S(2)}, u32[]{:S(2)}) collective-permute-start(f32[24,512]{1,0:T(8,128)S(1)} %get-tuple-element.45.own_ref), channel_id=1, source_target_pairs={{32,0},{64,32},{96,64},{128,96},{160,128},{192,160},{224,192},{256... | collective-permute-start | bytes 147464 | tf_op jit(solution)/shard_map/ppermute | solution.py:589
  25.9 55.9 %copy-start.2 = (f32[4,1,16,128]{3,2,1,0:T(8,128)S(1)}, f32[4,1,16,128]{3,2,1,0:T(8,128)}, u32[]{:S(2)}) copy-start(f32[4,1,16,128]{3,2,1,0:T(8,128)} %base_hbm.1) | copy-start | bytes 98308
  25.9 55.9 %copy-start.3 = (f32[4,1,16,128]{3,2,1,0:T(8,128)S(1)}, f32[4,1,16,128]{3,2,1,0:T(8,128)}, u32[]{:S(2)}) copy-start(f32[4,1,16,128]{3,2,1,0:T(8,128)} %mon_hbm.1) | copy-start | bytes 98308
  25.9 55.9 %copy-start.6 = (s32[4,1,2,2]{0,3,2,1:T(2,128)S(1)}, s32[4,1,2,2]{0,3,2,1:T(2,128)}, u32[]{:S(2)}) copy-start(s32[4,1,2,2]{0,3,2,1:T(2,128)} %param.8) | copy-start | bytes 196
